TPU v7x, 128 devices: a whole 4x4x4 slice. The times are simulated.
128 devices in a mesh: dp: 32 (over z, x_lo, y), ctx: 4 (over x_hi, core).
Axes of the slice: x: 4 (x_hi: 2, x_lo: 2; x = x_hi * 2 + x_lo), y: 4, z: 4, core: 2. Of those that a mesh axis runs over, the one named last changes fastest.
Arguments:
- tokens: bfloat16 [16384, 2048], P(('dp', 'ctx')), may hold values from -24 to 24
- cotangent: bfloat16 [16384, 2048], P(('dp', 'ctx')), may hold values from -6 to 6
- lengths: int32 [32, 2], P('dp'), may hold values from 1 to 448, 512 in all within a row
- span_ids: int32 [32, 8], P('dp'), may hold values from 0 to 7, each once within a row
- query_weight: float32 [2048, 2048], P(('dp', 'ctx')), may hold values from -0.125 to 0.125
- key_matrix: float32 [2048, 1024], P(('dp', 'ctx')), may hold values from -0.125 to 0.125
- value_matrix: float32 [2048, 1024], P(('dp', 'ctx')), may hold values from -0.125 to 0.125
- out_weight: float32 [2048, 2048], P(('dp', 'ctx')), may hold values from -1.5 to 1.5
- gate_weight: float32 [2048, 6144], P(('dp', 'ctx')), may hold values from -0.125 to 0.125
- up_weight: float32 [2048, 6144], P(('dp', 'ctx')), may hold values from -0.125 to 0.125
- down_weight: float32 [6144, 2048], P(('dp', 'ctx')), may hold values from -0.078125 to 0.078125
- norm_gains: float32 [4352], P(('dp', 'ctx')), may hold values from 0.5 to 1.5
- query_first: float32 [2048, 2048], P(('dp', 'ctx')), may hold values from -80 to 80
- key_first_moment: float32 [2048, 1024], P(('dp', 'ctx')), may hold values from -80 to 80
- value_first_moment: float32 [2048, 1024], P(('dp', 'ctx')), may hold values from -160 to 160
- out_first: float32 [2048, 2048], P(('dp', 'ctx')), may hold values from -6 to 6
- gate_first: float32 [2048, 6144], P(('dp', 'ctx')), may hold values from -24 to 24
- up_first: float32 [2048, 6144], P(('dp', 'ctx')), may hold values from -24 to 24
- down_first: float32 [6144, 2048], P(('dp', 'ctx')), may hold values from -48 to 48
- gains_first: float32 [4352], P(('dp', 'ctx')), may hold values from -128 to 128
- query_second: float32 [2048, 2048], P(('dp', 'ctx')), may hold values from 861.7984 to 3447.1936
- key_second_moment: float32 [2048, 1024], P(('dp', 'ctx')), may hold values from 861.7984 to 3447.1936
- value_second_moment: float32 [2048, 1024], P(('dp', 'ctx')), may hold values from 3447.1936 to 13788.774
- out_second: float32 [2048, 2048], P(('dp', 'ctx')), may hold values from 19.33312 to 77.49632
- gate_second: float32 [2048, 6144], P(('dp', 'ctx')), may hold values from 77.49632 to 309.6576
- up_second: float32 [2048, 6144], P(('dp', 'ctx')), may hold values from 77.49632 to 309.6576
- down_second: float32 [6144, 2048], P(('dp', 'ctx')), may hold values from 309.6576 to 1240.2688
- gains_second: float32 [4352], P(('dp', 'ctx')), may hold values from 1933.312 to 7749.632
Outputs:
- block_output: bfloat16 [16384, 2048], P(('dp', 'ctx'))
- input_grad: float32 [16384, 2048], P(('dp', 'ctx'))
- new_query_weight: float32 [2048, 2048], P(('dp', 'ctx'))
- new_query_first: float32 [2048, 2048], P(('dp', 'ctx'))
- new_query_second: float32 [2048, 2048], P(('dp', 'ctx'))
- new_key_weight: float32 [2048, 1024], P(('dp', 'ctx'))
- new_key_first: float32 [2048, 1024], P(('dp', 'ctx'))
- new_key_second: float32 [2048, 1024], P(('dp', 'ctx'))
- new_value_weight: float32 [2048, 1024], P(('dp', 'ctx'))
- new_value_first: float32 [2048, 1024], P(('dp', 'ctx'))
- new_value_second: float32 [2048, 1024], P(('dp', 'ctx'))
- new_out_weight: float32 [2048, 2048], P(('dp', 'ctx'))
- new_out_first: float32 [2048, 2048], P(('dp', 'ctx'))
- new_out_second: float32 [2048, 2048], P(('dp', 'ctx'))
- new_gate_weight: float32 [2048, 6144], P(('dp', 'ctx'))
- new_gate_first: float32 [2048, 6144], P(('dp', 'ctx'))
- new_gate_second: float32 [2048, 6144], P(('dp', 'ctx'))
- new_up_weight: float32 [2048, 6144], P(('dp', 'ctx'))
- new_up_first: float32 [2048, 6144], P(('dp', 'ctx'))
- new_up_second: float32 [2048, 6144], P(('dp', 'ctx'))
- new_down_weight: float32 [6144, 2048], P(('dp', 'ctx'))
- new_down_first: float32 [6144, 2048], P(('dp', 'ctx'))
- new_down_second: float32 [6144, 2048], P(('dp', 'ctx'))
- new_gains: float32 [4352], P(('dp', 'ctx'))
- new_gains_first: float32 [4352], P(('dp', 'ctx'))
- new_gains_second: float32 [4352], P(('dp', 'ctx'))
Inputs may be any that keep to these rules, and one draw needn't show every extreme that they name: Row g holds the lengths of the 2 sequences of data group g, laid end to end in this order over its 512 slots; they sum to 512. `span_ids`: entry 2 c + j of row g is the block of 64 slots held by block j of device c of data group g; each row names every block once.
All inputs are finite; a program needn't handle non-finite values.
Results may differ from a plain program's by a relative error of at most 0.02.
Values may be sent and summed in bfloat16 or wider, within the bound.
No kernel may reach another device: no remote copies, remote signals or barrier semaphores. Data moves between devices by JAX's collectives and lax.ppermute only.
A program may use at most 512 MiB of HBM per device.

v0:
```python
import math

import jax
import jax.numpy as jnp
import ml_dtypes
import numpy as np
from jax import lax
from jax.experimental import pallas as pl
from jax.experimental.pallas import tpu as pltpu
from jax.sharding import Mesh
from jax.sharding import PartitionSpec as P

MODEL_WIDTH = 2048
QUERY_HEADS = 16
KEY_VALUE_HEADS = 8
HEAD_SIZE = 128
FF = 6144
TOK_DEV = 128
STEP = 10

EPS = 1e-06
THETA = 1000000.0
BETA_ONE = 0.9
BETA_TWO = 0.95
ADAM_EPS = 1e-08
DECAY = 0.1

AXES = ("z", "xl", "y", "xh", "c")
SIZES = (4, 2, 4, 2, 2)
RING = ("xl", "xh", "c")
PLANE = ("z", "y")
CHIPS = ("xl", "xh")
SHARE = 8
OFFSETS = (0, 2, 1, 3)
BF = jnp.bfloat16
F32 = jnp.float32


def chip_number(x):
    return (x % 2) * 2 + x // 2


def from_chip(value, offset):
    pairs = [(chip_number((x + offset) % 4), chip_number(x)) for x in range(4)]
    return lax.ppermute(value, CHIPS, pairs)


def from_core(value):
    return lax.ppermute(value, "c", [(0, 1), (1, 0)])


def row_route():
    pairs = []
    for z in range(4):
        for xl in range(2):
            for y in range(4):
                for xh in range(2):
                    for c in range(2):
                        own = (((z * 2 + xl) * 4 + y) * 2 + xh) * 2 + c
                        part = 2 * z + xl
                        to = (((y * 2 + part // 4) * 4 + (xh * 2 + c)) * 2 + (part // 2) % 2) * 2 + part % 2
                        pairs.append((own, to))
    return pairs


def from_chips(block):
    return [block] + [from_chip(block, offset) for offset in OFFSETS[1:]]


def with_cores(near):
    return near + [from_core(value) for value in near]


def row_blocks():
    return [group * 4 + core * 2 + chip for core in range(2) for group in range(2) for chip in range(2)]


def dot(left, right):
    return jnp.dot(left, right, preferred_element_type=F32)


def dot_last(left, right):
    return lax.dot_general(left, right, (((1,), (1,)), ((), ())), preferred_element_type=F32)


def dot_first(left, right):
    return lax.dot_general(left, right, (((0,), (0,)), ((), ())), preferred_element_type=F32)


def inverse_rms(values):
    return lax.rsqrt(jnp.mean(values * values, axis=-1, keepdims=True) + EPS)


class Arriving:
    def __init__(self, source, buffer, sem):
        self.buffer, self.shape, self.here = buffer, buffer.shape, False
        self.copy = pltpu.make_async_copy(source, buffer, sem)

    def start(self):
        self.copy.start()

    def wait(self):
        if not self.here:
            self.copy.wait()
        self.here = True

    def __getitem__(self, index):
        self.wait()
        return self.buffer[index]


class Leaving:
    def __init__(self, buffer, target, sem):
        self.buffer, self.shape, self.sent = buffer, buffer.shape, False
        self.copy = pltpu.make_async_copy(buffer, target, sem)

    def __getitem__(self, index):
        return self.buffer[index]

    def __setitem__(self, index, value):
        self.buffer[index] = value

    def send(self):
        self.sent = True
        self.copy.start()


def bytes_of(values):
    return sum(math.prod(v.shape) * jnp.dtype(v.dtype).itemsize for v in values)


class Far:
    def __init__(self, value, later=False):
        self.value, self.later = value, later


HBM = pl.BlockSpec(memory_space=pltpu.HBM)
ANY = pl.BlockSpec(memory_space=pl.ANY)


def order_specs(after):
    return [HBM if isinstance(a, Far) else ANY for a in after], [a.value if isinstance(a, Far) else a for a in after]


def call(body, outs, args, after=(), scratch=(), flops=0, any_first=0, any_out=False, scalars=0, near=(), hidden=False, large=False, mark=False, name=None):
    if mark:
        outs = [*outs, shape((8, 128), F32)]
    after_specs, after = order_specs(after)
    far_in = [isinstance(a, Far) for a in args]
    later = [isinstance(a, Far) and a.later for a in args]
    far_out = [isinstance(o, Far) for o in outs]
    args = [a.value if isinstance(a, Far) else a for a in args]
    outs = [o.value if isinstance(o, Far) else o for o in outs]
    size = bytes_of((*args, *outs))
    held = bytes_of(args[any_first:]) + bytes_of(() if any_out else outs)
    held += bytes_of([v for v in scratch if v.memory_space == pltpu.VMEM])
    moved = [v for v, far in zip((*args, *outs), far_in + far_out) if far]
    n_in, n_out, n_move = len(args), len(outs), len(moved)

    def run(*refs):
        ins, refs = list(refs[:n_in]), refs[n_in + len(after) :]
        results, refs = list(refs[:n_out]), refs[n_out:]
        own, refs = refs[: len(scratch)], refs[len(scratch) :]
        buffers, sems = list(refs[:n_move]), list(refs[n_move:])
        for i, far in enumerate(far_in):
            if far:
                ins[i] = Arriving(ins[i], buffers.pop(0), sems.pop(0))
                if not later[i]:
                    ins[i].start()
        for i, far in enumerate(far_out):
            if far:
                results[i] = Leaving(buffers.pop(0), results[i], sems.pop(0))
        if mark:
            results[-1][...] = jnp.zeros((8, 128), F32)
        body(*ins, *(results[:-1] if mark else results), *own)
        for value in ins:
            if isinstance(value, Arriving):
                value.wait()
        for value in results:
            if isinstance(value, Leaving) and not value.sent:
                value.send()
        for value in results:
            if isinstance(value, Leaving):
                value.copy.wait()

    def spec(far):
        return HBM if far else pl.BlockSpec(memory_space=pltpu.VMEM)

    in_specs = [spec(far or (i < any_first and i not in near)) for i, far in enumerate(far_in)]
    in_specs[:scalars] = [pl.BlockSpec(memory_space=pltpu.SMEM)] * scalars

    return pl.pallas_call(
        run,
        out_shape=tuple(outs),
        in_specs=in_specs + after_specs,
        out_specs=tuple(spec(far or (any_out and i == 0)) for i, far in enumerate(far_out)),
        scratch_shapes=list(scratch)
        + [pltpu.VMEM(v.shape, v.dtype) for v in moved]
        + [pltpu.SemaphoreType.DMA for _ in moved],
        compiler_params=pltpu.CompilerParams(vmem_limit_bytes=large * 2**20 if large else held + 12 * 2**20),
        cost_estimate=pl.CostEstimate(flops=flops, bytes_accessed=0 if hidden else size, transcendentals=0),
        name=name,
    )(*args, *after)


def tie(values, after, name, spec=ANY):
    count = len(values)
    after_specs, after = order_specs(after)

    def body(*refs):
        pass

    return pl.pallas_call(
        body,
        out_shape=tuple(jax.ShapeDtypeStruct(v.shape, v.dtype) for v in values),
        in_specs=[spec] * count + after_specs,
        out_specs=tuple(spec for _ in values),
        input_output_aliases={i: i for i in range(count)},
        name=name,
    )(*values, *after)


def shape(dims, dtype=BF):
    return jax.ShapeDtypeStruct(tuple(dims), dtype)


class Sizes:
    def __init__(self):
        self.width = MODEL_WIDTH
        self.heads = QUERY_HEADS // SHARE
        self.query = self.heads * HEAD_SIZE
        self.cell = self.query + 2 * HEAD_SIZE
        self.hidden = FF // SHARE
        self.row = MODEL_WIDTH // 128
        self.down_row = FF // 128
        self.out_parts = self.width // self.cell
        self.mlp_parts = 2 * self.hidden // self.cell
        self.ring_rows = SHARE * self.row
        self.mlp_rows = self.mlp_parts * self.row
        self.out_rows = self.out_parts * self.row
        self.down_rows = self.out_parts * self.down_row
        self.early = self.ring_rows + self.out_rows + self.row
        self.late = SHARE * self.mlp_rows + self.down_rows
        self.gains = (2 * MODEL_WIDTH + 2 * HEAD_SIZE) // 128
        self.block = TOK_DEV
        self.rows = 8 * TOK_DEV
        self.group = 4 * TOK_DEV
        self.half = 2 * TOK_DEV


def pack_weights(s):
    def body(query, key, value, out, gate, up, down, gains, columns, lines):
        for j in range(SHARE):
            q, h = s.query, HEAD_SIZE
            columns[j, : s.row, :q] = query[:, j * q : (j + 1) * q].astype(BF)
            columns[j, : s.row, q : q + h] = key[:, j * h : (j + 1) * h].astype(BF)
            columns[j, : s.row, q + h :] = value[:, j * h : (j + 1) * h].astype(BF)
            for source, start in ((gate, 0), (up, s.hidden)):
                done = 0
                while done < s.hidden:
                    at = start + done
                    part, inside = at // s.cell, at % s.cell
                    size = min(s.cell - inside, s.hidden - done)
                    columns[j, s.row * (1 + part) : s.row * (2 + part), inside : inside + size] = source[
                        :, j * s.hidden + done : j * s.hidden + done + size
                    ].astype(BF)
                    done += size
            columns[j, s.row + s.mlp_rows :, :] = jnp.zeros((s.row, s.cell), BF)
            columns[j, s.row + s.mlp_rows :, : s.gains] = jnp.broadcast_to(gains[...], (s.row, s.gains)).astype(BF)
        for p in range(s.out_parts):
            lines[p * s.row : (p + 1) * s.row] = out[:, p * s.cell : (p + 1) * s.cell].astype(BF)
            at = s.out_rows + p * s.down_row
            lines[at : at + s.down_row] = down[:, p * s.cell : (p + 1) * s.cell].astype(BF)

    return body


def place_weights(s):
    def body(columns, lines, early, late, table):
        gain_at = s.row + s.mlp_rows
        table[...] = jnp.zeros_like(table)
        for j in range(SHARE):
            early[j * s.row : (j + 1) * s.row] = columns[j, : s.row]
            late[j * s.mlp_rows : (j + 1) * s.mlp_rows] = columns[j, s.row : gain_at]
            table[j : j + 1] = columns[j, gain_at : gain_at + s.row].astype(F32)[:1]
        early[s.ring_rows : s.ring_rows + s.out_rows] = lines[: s.out_rows]
        early[s.ring_rows + s.out_rows :] = table[...].astype(BF)
        late[SHARE * s.mlp_rows :] = lines[s.out_rows :]

    return body


def fill_head_weight(s, early, target):
    part = 4 * s.row
    for z in range(4):
        for xl in range(2):
            for y in range(4):
                at = ((z * 2 + xl) * 4 + y) * part
                target[at : at + part] = early[z * 4 + y, xl * part : (xl + 1) * part]


def fill_out_weight(s, early, target):
    for f in range(16):
        for p in range(s.out_parts):
            at = s.ring_rows + p * s.row
            target[f * s.row : (f + 1) * s.row, p * s.cell : (p + 1) * s.cell] = early[f, at : at + s.row]


def turn(value):
    return pltpu.roll(value, HEAD_SIZE // 2, 1)


def head_forward(s):
    scale = HEAD_SIZE ** (-0.5)

    def body(*refs):
        blocks = refs[:8]
        early, cosine, sine, bias, gain_one, gain_query, gain_key = refs[8:15]
        weight, out_weight, normed, linear, probs, query, key, value, mixed, near, far = refs[15:]
        for ref, at in zip(blocks, row_blocks()):
            wide = ref[...].astype(F32)
            normed[at * s.block : (at + 1) * s.block] = (wide * inverse_rms(wide) * gain_one[...]).astype(BF)
        normed.send()
        fill_head_weight(s, early, weight)
        weight.send()
        q, h = s.query, HEAD_SIZE
        for group in range(2):
            rows = pl.ds(group * s.group, s.group)
            lin = dot(normed[rows], weight[...])
            linear[rows] = lin[:, : q + h]
            value[rows] = lin[:, q + h :].astype(BF)
            cos, sin = cosine[rows], sine[rows]

            def turned(part, gain):
                part = part * inverse_rms(part) * gain[...]
                return (part * cos + turn(part) * sin).astype(BF)

            key[rows] = turned(lin[:, q : q + h], gain_key)
            for r in range(s.heads):
                query[rows, r * h : (r + 1) * h] = turned(lin[:, r * h : (r + 1) * h], gain_query)
        linear.send()
        fill_out_weight(s, early, out_weight)
        out_weight.send()
        for group in range(2):
            rows = pl.ds(group * s.group, s.group)
            for r in range(s.heads):
                score = dot_last(query[rows, r * h : (r + 1) * h], key[rows]) * scale + bias[group]
                expo = jnp.exp(score - jnp.max(score, axis=-1, keepdims=True))
                prob = expo * (1.0 / jnp.sum(expo, axis=-1, keepdims=True))
                probs[group * s.heads + r] = prob
                mixed[rows, r * h : (r + 1) * h] = dot(prob.astype(BF), value[rows]).astype(BF)
        probs.send()
        for target, core in ((far, 1), (near, 0)):
            for group in range(2):
                rows = pl.ds(group * s.group + core * s.half, s.half)
                target[pl.ds(group * s.half, s.half)] = dot(mixed[rows], out_weight[...]).astype(BF)
            if core:
                far.send()

    return body


def ring_add(s):
    def body(near, arrived, own, *others):
        own[...] = near[: s.block].astype(F32) + arrived[: s.block].astype(F32)
        for i, other in enumerate(others):
            rows = pl.ds((i + 1) * s.block, s.block)
            other[...] = (near[rows].astype(F32) + arrived[rows].astype(F32)).astype(BF)

    return body


def total_of(own, parts):
    total = own[...]
    for part in parts:
        total = total + part[...].astype(F32)
    return total


def branch_end(s):
    def body(own, first, second, third, tokens, gain_two, hidden_two, normed):
        value = tokens[...].astype(F32) + total_of(own, (first, second, third))
        hidden_two[...] = value
        normed[...] = (value * inverse_rms(value) * gain_two[...]).astype(BF)

    return body


def norm_back(values, gain, grad):
    scale = inverse_rms(values)
    normalized = values * scale
    inner = grad * gain
    back = scale * inner - normalized * scale * jnp.mean(inner * normalized, axis=-1, keepdims=True)
    return back, grad * normalized


def gather_into(s, blocks, buffer, sems):
    copies = {}
    for i, (ref, at) in enumerate(zip(blocks, row_blocks())):
        copies[at] = pltpu.make_async_copy(ref, buffer.at[pl.ds(at * s.block, s.block)], sems.at[i])
        copies[at].start()
    return copies


def wait_all(copies):
    for copy in copies.values():
        copy.wait()


def mlp_block(s):
    step = 2 * HEAD_SIZE

    def body(*refs):
        blocks, upstream_blocks, gathered = refs[:8], refs[8:16], refs[16]
        down, hidden, grads, far, near, normed, upstream, weight, grad_hidden, late, sems, up_sems, late_sems = refs[17:]
        copies = gather_into(s, upstream_blocks, upstream, up_sems)
        split = SHARE * s.mlp_rows
        arriving = []
        for i, rows in enumerate((pl.ds(split, s.down_rows), pl.ds(0, split))):
            arriving.append(pltpu.make_async_copy(gathered.at[:, rows], late.at[:, rows], late_sems.at[i]))
            arriving[i].start()
        normed_copies = gather_into(s, blocks, normed, sems)
        arriving[0].wait()
        for f in range(16):
            for p in range(s.out_parts):
                start = SHARE * s.mlp_rows + p * s.down_row
                down[f * s.down_row : (f + 1) * s.down_row, p * s.cell : (p + 1) * s.cell] = late[
                    f, start : start + s.down_row
                ]
        down.send()
        wait_all(copies)
        for n in range(s.hidden // step):
            columns = slice(n * step, (n + 1) * step)
            grad_hidden[:, columns] = dot_last(upstream[...], down[columns])
        arriving[1].wait()
        for f in range(16):
            z, y = divmod(f, 4)
            for j in range(SHARE):
                xl, part = divmod(j, 4)
                at = (((z * 2 + xl) * 4 + y) * 4 + part) * s.row
                for p in range(s.mlp_parts):
                    start = j * s.mlp_rows + p * s.row
                    weight[at : at + s.row, p * s.cell : (p + 1) * s.cell] = late[f, start : start + s.row]
        wait_all(normed_copies)
        for n in range(s.hidden // step):
            columns = slice(n * step, (n + 1) * step)
            second = slice(s.hidden + n * step, s.hidden + (n + 1) * step)
            gate = dot(normed[...], weight[:, columns])
            up = dot(normed[...], weight[:, second])
            sigma = jax.nn.sigmoid(gate)
            active = gate * sigma
            hidden[:, columns] = (active * up).astype(BF)
            grad = grad_hidden[:, columns]
            grads[:, columns] = (grad * up * (sigma * (1.0 + gate * (1.0 - sigma)))).astype(BF)
            grads[:, second] = (grad * active).astype(BF)
        hidden.send()
        grads.send()
        for target, core in ((far, 1), (near, 0)):
            for n in range(s.width // step):
                columns = slice(n * step, (n + 1) * step)
                for group in range(2):
                    rows = pl.ds(group * s.group + core * s.half, s.half)
                    part = dot_last(grads[rows], weight[columns])
                    target[pl.ds(group * s.half, s.half), columns] = part.astype(BF)
            target.send()

    return body


def mlp_weight_grads(s):
    step = 4 * s.row * 4

    def body(*refs):
        normed_blocks, blocks = refs[:8], refs[8:16]
        grads, hidden, target, normed, upstream, made, normed_sems, sems, out_sems = refs[16:]
        normed_copies = gather_into(s, normed_blocks, normed, normed_sems)
        copies = gather_into(s, blocks, upstream, sems)
        leaving = []
        grads.start()
        hidden.start()
        wait_all(normed_copies)
        for z in range(4):
            for xl in range(2):
                at = (z * 2 + xl) * step
                tile = dot_first(normed[:, at : at + step], grads[...]).astype(BF)
                for y in range(4):
                    for part in range(4):
                        line = (y * 4 + part) * s.row
                        for p in range(s.mlp_parts):
                            start = (xl * 4 + part) * s.mlp_rows + p * s.row
                            made[z * 4 + y, start : start + s.row] = tile[
                                line : line + s.row, p * s.cell : (p + 1) * s.cell
                            ]
            if z % 2:
                pair = z // 2
                if pair == 0:
                    wait_all(copies)
                wide = s.hidden // 2
                columns = hidden[:, pair * wide : (pair + 1) * wide]
                for p in range(s.out_parts):
                    tile = dot_first(columns, upstream[:, p * s.cell : (p + 1) * s.cell]).astype(BF)
                    for f in range(8):
                        start = SHARE * s.mlp_rows + p * s.down_row
                        made[pair * 8 + f, start : start + s.down_row] = tile[f * s.down_row : (f + 1) * s.down_row]
                half = pl.ds(pair * 8, 8)
                copy = pltpu.make_async_copy(made.at[half], target.at[half], out_sems.at[pair])
                copy.start()
                leaving.append(copy)
        for copy in leaving:
            copy.wait()

    return body


def mlp_out(s):
    step = 4 * HEAD_SIZE

    def body(hidden, down, near, far):
        for target, core in ((far, 1), (near, 0)):
            for group in range(2):
                rows = pl.ds(group * s.group + core * s.half, s.half)
                for n in range(s.width // step):
                    columns = slice(n * step, (n + 1) * step)
                    target[pl.ds(group * s.half, s.half), columns] = dot(hidden[rows], down[:, columns]).astype(BF)

    return body


def mlp_back_end(s):
    def body(own, first, second, third, cotangent, hidden_two, gain_two, grad_hidden_two, low, terms):
        grad = total_of(own, (first, second, third))
        back, gains = norm_back(hidden_two[...], gain_two[...], grad)
        value = cotangent[...].astype(F32) + back
        grad_hidden_two[...] = value
        low[...] = value.astype(BF)
        terms[...] = jnp.sum(gains, axis=0, keepdims=True)

    return body


def out_weight_grads(s):
    def body(*refs):
        mixed, out_grad, branch, sems = refs[8:]
        wait_all(gather_into(s, refs[:8], branch, sems))
        for p in range(s.out_parts):
            columns = slice(p * s.cell, (p + 1) * s.cell)
            out_grad[:, columns] = dot_first(mixed[...], branch[:, columns]).astype(BF)

    return body


def head_back(s):
    scale = HEAD_SIZE ** (-0.5)

    def body(*refs):
        blocks = refs[:8]
        out_weight, probs, linear, cosine, sine, query, key, value, normed, weight = refs[8:18]
        gain_query, gain_key, gain_one, gain_two_terms, owner, lane = refs[18:24]
        near, far, owned_rows, branch, grad_mixed, grads, gain_row, sems = refs[24:]
        copies = gather_into(s, blocks, branch, sems)
        for later in (out_weight, probs, linear, cosine, sine, query, key, value, normed, weight):
            later.start()
        q, h = s.query, HEAD_SIZE
        query_sum = jnp.zeros((1, h), F32)
        key_sum = jnp.zeros((1, h), F32)
        for group in range(2):
            rows = pl.ds(group * s.group, s.group)
            for at in range(group * 4, group * 4 + 4):
                copies[at].wait()
            grad_mixed[rows] = dot_last(branch[rows], out_weight[...]).astype(BF)
            cos, sin = cosine[rows], sine[rows]
            key_grad = jnp.zeros((s.group, h), F32)
            value_grad = jnp.zeros((s.group, h), F32)
            for r in range(s.heads):
                columns = slice(r * h, (r + 1) * h)
                prob = probs[group * s.heads + r]
                out = grad_mixed[rows, columns]
                grad_prob = dot_last(out, value[rows])
                inner = jnp.sum(prob * grad_prob, axis=-1, keepdims=True)
                grad_score = (prob * (grad_prob - inner)).astype(BF)
                value_grad = value_grad + dot_first(prob.astype(BF), out)
                key_grad = key_grad + dot_first(grad_score, query[rows, columns]) * scale
                turned = dot(grad_score, key[rows]) * scale
                back, terms = norm_back(
                    linear[rows, columns], gain_query[...], turned * cos - turn(turned) * sin
                )
                grads[rows, columns] = back.astype(BF)
                query_sum = query_sum + jnp.sum(terms, axis=0, keepdims=True)
            back, terms = norm_back(
                linear[rows, q : q + h], gain_key[...], key_grad * cos - turn(key_grad) * sin
            )
            grads[rows, q : q + h] = back.astype(BF)
            key_sum = key_sum + jnp.sum(terms, axis=0, keepdims=True)
            grads[rows, q + h :] = value_grad.astype(BF)
        wide = 4 * HEAD_SIZE
        for n in range(s.width // wide):
            columns = slice(n * wide, (n + 1) * wide)
            total = jnp.zeros((1, wide), F32)
            for target, core in ((far, 1), (near, 0)):
                for group in range(2):
                    rows = pl.ds(group * s.group + core * s.half, s.half)
                    part = dot_last(grads[rows], weight[columns])
                    target[pl.ds(group * s.half, s.half), columns] = part.astype(BF)
                    total = total + jnp.sum(part * normed[rows, columns].astype(F32), axis=0, keepdims=True)
            gain_row[:, columns] = total / gain_one[:, columns]
        far.send()
        near.send()
        gain_row[:, s.width : 2 * s.width] = gain_two_terms[...]
        gain_row[:, 2 * s.width : 2 * s.width + h] = query_sum
        gain_row[:, 2 * s.width + h :] = key_sum
        owned = dot((owner[...].astype(F32) * gain_row[...]).astype(BF), lane[...])
        for o in range(128):
            owned_rows[o, :, s.cell :] = jnp.broadcast_to(owned[o : o + 1], (s.row, h)).astype(BF)
        step = 16 * s.row
        for n in range(8):
            tile = dot_first(normed[:, n * step : (n + 1) * step], grads[...]).astype(BF)
            owned_rows[n * 16 : (n + 1) * 16, :, : s.cell] = tile.reshape(16, s.row, s.cell)

    return body


def plane_sum(s):
    def body(parts, total):
        value = parts[0].astype(F32)
        for f in range(1, 16):
            value = value + parts[f].astype(F32)
        total[...] = value.astype(BF)

    return body


def input_end(s):
    def body(own, first, second, third, tokens, grad_hidden_two, gain_one, input_grad):
        back, _ = norm_back(tokens[...].astype(F32), gain_one[...], total_of(own, (first, second, third)))
        input_grad[...] = grad_hidden_two[...] + back

    return body


def output_end(s):
    def body(own, first, second, third, hidden_two, block_output):
        block_output[...] = (hidden_two[...] + total_of(own, (first, second, third))).astype(BF)

    return body


def adam(weight, grad, first, second, rate, decay):
    first_new = BETA_ONE * first + (1.0 - BETA_ONE) * grad
    second_new = BETA_TWO * second + (1.0 - BETA_TWO) * grad * grad
    first_hat = first_new / (1.0 - BETA_ONE**STEP)
    second_hat = second_new / (1.0 - BETA_TWO**STEP)
    weight_new = weight - rate * (first_hat / (jnp.sqrt(second_hat) + ADAM_EPS) + decay * weight)
    return (weight_new, first_new, second_new)


def step_into(ins, outs, columns, grad, rate, decay):
    results = adam(ins[0][:, columns], grad.astype(F32), ins[1][:, columns], ins[2][:, columns], rate, decay)
    for out, value in zip(outs, results):
        out[:, columns] = value


def split_refs(refs, first, count):
    ins = [refs[first + 3 * i : first + 3 * i + 3] for i in range(count)]
    outs = [refs[first + 3 * (count + i) : first + 3 * (count + i) + 3] for i in range(count)]
    return ins, outs


def send_all(outs):
    for out in outs:
        out.send()


def head_update(s):
    def body(*refs):
        owned, lines = refs[:2]
        ins, outs = split_refs(refs, 2, 5)
        rate = MODEL_WIDTH ** (-0.5)
        out_rate = (TOK_DEV / (QUERY_HEADS * HEAD_SIZE)) ** 0.5
        gain_grad = jnp.zeros((s.row, HEAD_SIZE), F32)
        for j in range(SHARE):
            xl, part = divmod(j, 4)
            grad = jnp.zeros((s.row, s.cell), F32)
            for z in range(4):
                for y in range(4):
                    source = ((z * 2 + xl) * 4 + y) * 4 + part
                    grad = grad + owned[source, :, : s.cell].astype(F32)
                    gain_grad = gain_grad + owned[source, :, s.cell :].astype(F32)
            start = 0
            for i, size in enumerate((s.query, HEAD_SIZE, HEAD_SIZE)):
                columns = slice(j * size, (j + 1) * size)
                step_into(ins[i], outs[i], columns, grad[:, start : start + size], rate, DECAY)
                start += size
        for i in range(3):
            send_all(outs[i])
        for p in range(s.out_parts):
            columns = slice(p * s.cell, (p + 1) * s.cell)
            step_into(ins[3], outs[3], columns, lines[:, columns], out_rate, DECAY)
        send_all(outs[3])
        step_into(ins[4], outs[4], slice(0, s.gains), gain_grad[:1, : s.gains], 0.5, 0.0)

    return body


def mlp_update(s):
    def body(*refs):
        columns, lines = refs[:2]
        ins, outs = split_refs(refs, 2, 3)
        for i, start in ((0, 0), (1, s.hidden)):
            for j in range(SHARE):
                done = 0
                while done < s.hidden:
                    at = start + done
                    part, inside = at // s.cell, at % s.cell
                    size = min(s.cell - inside, s.hidden - done)
                    grad = columns[j, part * s.row : (part + 1) * s.row, inside : inside + size]
                    own = slice(j * s.hidden + done, j * s.hidden + done + size)
                    step_into(ins[i], outs[i], own, grad, MODEL_WIDTH ** (-0.5), DECAY)
                    done += size
            send_all(outs[i])
        for p in range(s.out_parts):
            grad = lines[p * s.down_row : (p + 1) * s.down_row]
            step_into(ins[2], outs[2], slice(p * s.cell, (p + 1) * s.cell), grad, FF ** (-0.5), DECAY)

    return body


def layout(table, other):
    span = TOK_DEV // 2
    both = jnp.stack([table, other])
    sizes, spans = both[:, :2], both[:, 2:]
    chip = lax.axis_index("xh") * 2 + lax.axis_index("xl")
    core = lax.axis_index("c")
    offset = jnp.arange(2)[:, None, None] + 2 * jnp.arange(2)[None, None, :]
    place = ((chip + offset) % 4) // 2 * 2 + (core + jnp.arange(2)[None, :, None]) % 2
    block = (2 * place[..., None] + jnp.arange(2)).reshape(2, 8)
    owner = jnp.sum(jnp.where(block[:, :, None] == jnp.arange(8), spans[:, None, :], 0), axis=-1)
    slots = (owner[:, :, None] * span + jnp.arange(span)).reshape(2, -1)
    ends = jnp.cumsum(sizes, axis=1)
    passed = slots[:, :, None] >= ends[:, None, :]
    sequence = jnp.sum(passed.astype(jnp.int32), axis=-1)
    position = slots - jnp.sum(jnp.where(passed, sizes[:, None, :], 0), axis=-1)
    return slots, sequence, position


def local(
    tokens,
    cotangent,
    lengths,
    span_ids,
    query_weight,
    key_matrix,
    value_matrix,
    out_weight,
    gate_weight,
    up_weight,
    down_weight,
    norm_gains,
    query_first,
    key_first_moment,
    value_first_moment,
    out_first,
    gate_first,
    up_first,
    down_first,
    gains_first,
    query_second,
    key_second_moment,
    value_second_moment,
    out_second,
    gate_second,
    up_second,
    down_second,
    gains_second,
):
    s = Sizes()
    block = (s.block, s.width)
    half_rows = (s.group, s.width)

    def ring_scatter(near, arrived, name, after=()):
        own, *others = call(
            ring_add(s), [shape(block, F32)] + [shape(block)] * 3, [near, arrived], after=after, name=name + "_add"
        )
        arrived = [from_chip(piece, -OFFSETS[i + 1]) for i, piece in enumerate(others)]
        return [own] + arrived, others

    columns, lines, mark = call(
        pack_weights(s),
        [shape((SHARE, 2 * s.row + s.mlp_rows, s.cell)), shape((s.out_rows + s.down_rows, s.cell))],
        [Far(query_weight), Far(key_matrix), Far(value_matrix), Far(out_weight), Far(gate_weight), Far(up_weight)]
        + [Far(down_weight), norm_gains[None]],
        large=54,
        mark=True,
        name="pack_weights",
    )
    (table,) = tie([jnp.concatenate([lengths[0], span_ids[0]])], [mark], "table_then")
    other_table = lax.ppermute(table, "xl", [(0, 1), (1, 0)])
    (tokens_then,) = tie([tokens], [mark], "tokens_then", HBM)
    input_near = from_chips(tokens_then)
    inputs = with_cores(input_near)
    columns = lax.all_to_all(columns, RING, 0, 0, tiled=True)
    lines = lax.ppermute(lines, AXES, row_route())

    count = 128 * s.gains
    owner = np.asarray(np.arange(count)[None] // s.gains == np.arange(128)[:, None], ml_dtypes.bfloat16)
    lane = np.asarray(np.arange(count)[:, None] % s.gains == np.arange(HEAD_SIZE)[None], ml_dtypes.bfloat16)

    early, late = call(
        place_weights(s),
        [shape((s.early, s.cell)), shape((s.late, s.cell))],
        [columns, lines],
        after=[other_table],
        scratch=[pltpu.VMEM((s.row, s.cell), F32)],
        name="place_weights",
    )
    early = lax.all_gather(early, PLANE, axis=0)
    (cotangent_then,) = tie([cotangent], [Far(input_near[1])], "cotangent_then", HBM)
    upstream_near = from_chips(cotangent_then)
    slots, sequence, position = layout(table, other_table)
    freq = THETA ** (-(2.0 * jnp.arange(HEAD_SIZE // 2, dtype=F32)) / HEAD_SIZE)
    angle = position.reshape(-1).astype(F32)[:, None] * freq
    cosine, sine = jnp.cos(angle), jnp.sin(angle)
    cosine = jnp.concatenate([cosine, cosine], axis=1)
    sine = jnp.concatenate([-sine, sine], axis=1)
    allowed = (sequence[:, :, None] == sequence[:, None, :]) & (slots[:, None, :] <= slots[:, :, None])
    bias = jnp.where(allowed, 0.0, -1e30).astype(F32)

    (late,) = tie(
        [late], [*inputs[1:], *upstream_near[1:], cosine, sine, bias], "late_then", HBM
    )
    late = lax.all_gather(late, PLANE, axis=0)
    upstream = with_cores(upstream_near)

    gain_at = s.ring_rows + s.out_rows
    gains = early[:, gain_at : gain_at + SHARE, : s.gains].astype(F32)
    gains = gains.reshape(4, 4, 2, -1).transpose(0, 2, 1, 3).reshape(1, -1)
    gain_one = gains[:, : s.width]
    gain_two = gains[:, s.width : 2 * s.width]
    gain_query = gains[:, 2 * s.width : 2 * s.width + HEAD_SIZE]
    gain_key = gains[:, 2 * s.width + HEAD_SIZE :]

    eight = pltpu.SemaphoreType.DMA((8,))
    head_weight, out_slice, normed_one, linear, probs, query, key, value, mixed, near, far = call(
        head_forward(s),
        [
            Far(shape((s.width, s.cell))),
            Far(shape((s.query, s.width))),
            Far(shape((s.rows, s.width))),
            Far(shape((s.rows, s.query + HEAD_SIZE), F32)),
            Far(shape((2 * s.heads, s.group, s.group), F32)),
            shape((s.rows, s.query)),
            shape((s.rows, HEAD_SIZE)),
            shape((s.rows, HEAD_SIZE)),
            shape((s.rows, s.query)),
            shape(half_rows),
            Far(shape(half_rows)),
        ],
        [*[Far(v) for v in inputs], Far(early), Far(cosine), Far(sine), Far(bias), gain_one, gain_query, gain_key],
        flops=2 * s.rows * s.width * (s.cell + s.query),
        large=54,
        name="head_forward",
    )
    parts, _ = ring_scatter(near, from_core(far), "branch")
    hidden_two, normed_two = call(
        branch_end(s), [shape(block, F32), shape(block)], [*parts, tokens, gain_two], name="branch_end"
    )
    normed_blocks = with_cores(from_chips(normed_two))
    down, hidden, grads, far, near = call(
        mlp_block(s),
        [
            Far(shape((s.hidden, s.width))),
            Far(shape((s.rows, s.hidden))),
            Far(shape((s.rows, 2 * s.hidden))),
            Far(shape(half_rows)),
            Far(shape(half_rows)),
        ],
        [*normed_blocks, *upstream, late],
        any_first=17,
        near=(0,),
        scratch=[
            pltpu.VMEM((s.rows, s.width), BF),
            pltpu.VMEM((s.rows, s.width), BF),
            pltpu.VMEM((s.width, 2 * s.hidden), BF),
            pltpu.VMEM((s.rows, s.hidden), F32),
            pltpu.VMEM((16, s.late, s.cell), BF),
            eight,
            eight,
            pltpu.SemaphoreType.DMA((2,)),
        ],
        flops=10 * s.rows * s.width * s.hidden,
        large=60,
        name="mlp_block",
    )
    parts, sent = ring_scatter(near, from_core(far), "mlp_back")
    late_grad, mark = call(
        mlp_weight_grads(s),
        [shape((16, s.late, s.cell))],
        [*normed_blocks, *upstream, Far(grads, later=True), Far(hidden, later=True)],
        any_first=16,
        near=(0,),
        any_out=True,
        after=sent,
        scratch=[
            pltpu.VMEM((s.rows, s.width), BF),
            pltpu.VMEM((s.rows, s.width), BF),
            pltpu.VMEM((16, s.late, s.cell), BF),
            eight,
            eight,
            pltpu.SemaphoreType.DMA((2,)),
        ],
        flops=6 * s.rows * s.width * s.hidden,
        large=54,
        mark=True,
        name="mlp_weight_grads",
    )
    grad_hidden_two, grad_branch, gain_two_terms = call(
        mlp_back_end(s),
        [shape(block, F32), shape(block), shape((1, s.width), F32)],
        [*parts, cotangent, hidden_two, gain_two],
        after=[mark],
        name="mlp_back_end",
    )
    (late_grad,) = tie([late_grad], [grad_branch], "late_grad_then", HBM)
    late_grad = lax.psum_scatter(late_grad.reshape(-1, s.cell), PLANE, scatter_dimension=0, tiled=True)
    branch_near = from_chips(grad_branch)
    out_near, out_far = call(
        mlp_out(s),
        [shape(half_rows)] * 2,
        [Far(hidden), Far(down)],
        after=[grad_branch],
        flops=2 * s.rows * s.width * s.hidden,
        large=54,
        name="mlp_out",
    )
    out_far, *branch_near[1:] = tie([out_far, *branch_near[1:]], [], "branch_then")
    branch_blocks = with_cores(branch_near)
    output_parts, out_sent = ring_scatter(out_near, from_core(out_far), "output")

    moved = (out_slice, probs, linear, cosine, sine, query, key, value, normed_one, head_weight)
    (out_grad,) = call(
        out_weight_grads(s),
        [Far(shape((s.query, s.width)))],
        [*branch_blocks, Far(mixed)],
        any_first=8,
        near=(0,),
        scratch=[pltpu.VMEM((s.rows, s.width), BF), eight],
        flops=2 * s.rows * s.width * s.query,
        large=54,
        name="out_weight_grads",
    )
    out_parts = lax.all_to_all(out_grad.reshape(16, s.row, s.width), PLANE, 0, 0, tiled=True)
    near, far, owned, mark = call(
        head_back(s),
        [
            Far(shape(half_rows)),
            Far(shape(half_rows)),
            Far(shape((128, s.row, s.cell + HEAD_SIZE))),
        ],
        [*branch_blocks, *[Far(v, later=True) for v in moved]]
        + [gain_query, gain_key, gain_one, gain_two_terms, owner, lane],
        any_first=8,
        near=(0,),
        after=out_sent,
        scratch=[
            pltpu.VMEM((s.rows, s.width), BF),
            pltpu.VMEM((s.rows, s.query), BF),
            pltpu.VMEM((s.rows, s.cell), BF),
            pltpu.VMEM((1, count), F32),
            eight,
        ],
        hidden=True,
        large=54,
        mark=True,
        name="head_back",
    )
    (block_output,) = call(output_end(s), [shape(block)], [*output_parts, hidden_two], name="output_end")
    (out_lines,) = call(plane_sum(s), [shape((s.row, s.width))], [out_parts], after=[mark], name="plane_sum")
    owned, far = tie([owned, far], [block_output, out_lines], "head_grads_then")
    owned = lax.all_to_all(owned, AXES, 0, 0, tiled=True)
    parts, sent = ring_scatter(near, from_core(far), "input")
    (late_grad,) = tie([late_grad], sent[:1], "late_grad_last")
    input_grad, input_mark = call(
        input_end(s), [shape(block, F32)], [*parts, tokens, grad_hidden_two, gain_one], mark=True, name="input_end"
    )

    home = [(to, own) for own, to in row_route()]
    mlp_end = SHARE * s.mlp_rows
    columns = lax.all_to_all(late_grad[:mlp_end].reshape(SHARE, s.mlp_rows, s.cell), RING, 0, 0, tiled=True)
    lines = lax.ppermute(late_grad[mlp_end:], AXES, home)
    out_lines = lax.ppermute(out_lines, AXES, home)

    def states(*groups):
        return [Far(a) for group in groups for a in group]

    mlp_states = states(
        (gate_weight, gate_first, gate_second),
        (up_weight, up_first, up_second),
        (down_weight, down_first, down_second),
    )
    mlp_new = call(
        mlp_update(s),
        [Far(shape(a.value.shape, F32)) for a in mlp_states],
        [columns, lines] + mlp_states,
        after=[Far(owned), input_mark],
        mark=True,
        large=62,
        name="mlp_update",
    )
    head_states = states(
        (query_weight, query_first, query_second),
        (key_matrix, key_first_moment, key_second_moment),
        (value_matrix, value_first_moment, value_second_moment),
        (out_weight, out_first, out_second),
    )
    gains_state = [a[None] for a in (norm_gains, gains_first, gains_second)]
    head_new = call(
        head_update(s),
        [Far(shape(a.value.shape, F32)) for a in head_states] + [shape(a.shape, F32) for a in gains_state],
        [owned, out_lines] + head_states + gains_state,
        after=[mlp_new[-1]],
        large=62,
        name="head_update",
    )
    return (block_output, input_grad, *head_new[:12], *mlp_new[:9], *[value[0] for value in head_new[12:]])


def solution(mesh):
    fine = Mesh(mesh.devices.reshape(SIZES), AXES)
    matrix, vector, grouped = P(AXES, None), P(AXES), P(("z", "xl", "y"), None)
    states = (matrix,) * 7 + (vector,)
    return jax.shard_map(
        local,
        mesh=fine,
        in_specs=(matrix, matrix, grouped, grouped) + states * 3,
        out_specs=(matrix, matrix) + (matrix,) * 21 + (vector,) * 3,
        check_vma=False,
    )
```

profile of v0, /device:TPU:6, one launch (start us, length us, event | category | flops | bytes accessed | tf_op | source)
XLA Modules:
  0.0 426.3 jit_solution(6136658112559991646)
XLA Ops:
  7.2 3.1 pack_weights.1
  10.4 4.9 %all-to-all-start = ((bf16[8,80,512]{2,1,0:T(8,128)(2,1)}), bf16[8,80,512]{2,1,0:T(8,128)(2,1)S(1)}, u32[]{:S(2)}, u32[]{:S(2)}) async-start(bf16[8,80,512]{2,1,0:T(8,128)(2,1)} %get-tuple-element.110), calls=%async_computation | async-start | bytes 1310720 | tf_op jit(solution)/shard_map/all_to_all | solution.py:800
  15.3 4.6 %collective-permute-start.7 = (bf16[256,512]{1,0:T(8,128)(2,1)}, bf16[256,512]{1,0:T(8,128)(2,1)S(1)}, u32[]{:S(2)}, u32[]{:S(2)}) collective-permute-start(bf16[256,512]{1,0:T(8,128)(2,1)} %get-tuple-element.111), channel_id=1, source_target_pairs={{0,0},{1,4},{2,8},{3,12},{4,32},{5,36},{6,40},{7,44},{8,64},{9,68}... | collective-permute-start | bytes 786440 | tf_op jit(solution)/shard_map/ppermute | solution.py:801
  21.4 8.7 %collective-permute-done.8.refs_2_ = s32[10]{0:T(128)S(1)} collective-permute-done((s32[10]{0:T(128)}, s32[10]{0:T(128)S(1)}, u32[]{:S(2)}, u32[]{:S(2)}) %collective-permute-start.8) | collective-permute-done | bytes 72 | tf_op jit(solution)/shard_map/ppermute | solution.py:796
  30.0 8.6 %collective-permute-done.7.refs_1_ = bf16[256,512]{1,0:T(8,128)(2,1)S(1)} collective-permute-done((bf16[256,512]{1,0:T(8,128)(2,1)}, bf16[256,512]{1,0:T(8,128)(2,1)S(1)}, u32[]{:S(2)}, u32[]{:S(2)}) %collective-permute-start.7) | collective-permute-done | bytes 262176 | tf_op jit(solution)/shard_map/ppermute | solution.py:801
  41.1 2.0 collective-permute-start.1
  44.9 11.2 %collective-permute-done.2.refs_3_ = bf16[128,2048]{1,0:T(8,128)(2,1)} collective-permute-done((bf16[128,2048]{1,0:T(8,128)(2,1)}, bf16[128,2048]{1,0:T(8,128)(2,1)}, u32[]{:S(2)}, u32[]{:S(2)}) %collective-permute-start.2) | collective-permute-done | bytes 524320 | tf_op jit(solution)/shard_map/ppermute | solution.py:45
  56.5 9.8 %collective-permute-done.refs_1_ = bf16[128,2048]{1,0:T(8,128)(2,1)S(1)} collective-permute-done((bf16[128,2048]{1,0:T(8,128)(2,1)}, bf16[128,2048]{1,0:T(8,128)(2,1)S(1)}, u32[]{:S(2)}, u32[]{:S(2)}) %collective-permute-start) | collective-permute-done | bytes 524320 | tf_op jit(solution)/shard_map/ppermute | solution.py:45
  67.0 3.3 collective-permute-start.22
  70.3 2.6 collective-permute-start.20
  74.3 1.9 fusion
  79.1 13.9 %collective-permute-done.22.refs_10_.refs_11_ = bf16[128,2048]{1,0:T(8,128)(2,1)S(1)} collective-permute-done((bf16[128,2048]{1,0:T(8,128)(2,1)}, bf16[128,2048]{1,0:T(8,128)(2,1)S(1)}, u32[]{:S(2)}, u32[]{:S(2)}) %collective-permute-start.22) | collective-permute-done | bytes 524320 | tf_op jit(solution)/shard_map/ppermute | solution.py:45
  93.0 3.3 collective-permute-done.21.refs_9_.refs_10_
  99.5 14.0 %head_forward.1 = (bf16[2048,512]{1,0:T(8,128)(2,1)}, bf16[256,2048]{1,0:T(8,128)(2,1)}, bf16[1024,2048]{1,0:T(8,128)(2,1)}, f32[1024,384]{1,0:T(8,128)}, f32[4,...) custom-call(bf16[128,2048]{1,0:T(8,128)(2,1)} %tokens_then.1.refs_0_, ...), custom_call_target="tpu_custom_call" | custom-call | flops 3221225472 | bytes 29631488 | tf_op jit(solution)/shard_map/head_forward/pallas_call | solution.py:192
  113.6 4.4 %collective-permute-done.9.refs_1_ = bf16[512,2048]{1,0:T(8,128)(2,1)S(1)} collective-permute-done((bf16[512,2048]{1,0:T(8,128)(2,1)}, bf16[512,2048]{1,0:T(8,128)(2,1)S(1)}, u32[]{:S(2)}, u32[]{:S(2)}) %collective-permute-start.9) | collective-permute-done | bytes 2097184 | tf_op jit(solution)/shard_map/ppermute | solution.py:49
  122.7 13.7 %collective-permute-done.10.refs_1_ = bf16[128,2048]{1,0:T(8,128)(2,1)S(1)} collective-permute-done((bf16[128,2048]{1,0:T(8,128)(2,1)S(1)}, bf16[128,2048]{1,0:T(8,128)(2,1)S(1)}, u32[]{:S(2)}, u32[]{:S(2)}) %collective-permute-start.10) | collective-permute-done | bytes 524320 | tf_op jit(solution)/shard_map/ppermute | solution.py:45
  136.4 8.2 %collective-permute-done.11.refs_2_ = bf16[128,2048]{1,0:T(8,128)(2,1)S(1)} collective-permute-done((bf16[128,2048]{1,0:T(8,128)(2,1)S(1)}, bf16[128,2048]{1,0:T(8,128)(2,1)S(1)}, u32[]{:S(2)}, u32[]{:S(2)}) %collective-permute-start.11) | collective-permute-done | bytes 524320 | tf_op jit(solution)/shard_map/ppermute | solution.py:45
  144.6 2.2 collective-permute-done.12.refs_3_
  150.3 11.9 %collective-permute-done.15.refs_3_ = bf16[128,2048]{1,0:T(8,128)(2,1)S(1)} collective-permute-done((bf16[128,2048]{1,0:T(8,128)(2,1)S(1)}, bf16[128,2048]{1,0:T(8,128)(2,1)S(1)}, u32[]{:S(2)}, u32[]{:S(2)}) %collective-permute-start.15) | collective-permute-done | bytes 524320 | tf_op jit(solution)/shard_map/ppermute | solution.py:45
  162.2 11.7 %collective-permute-done.14.refs_2_ = bf16[128,2048]{1,0:T(8,128)(2,1)S(1)} collective-permute-done((bf16[128,2048]{1,0:T(8,128)(2,1)S(1)}, bf16[128,2048]{1,0:T(8,128)(2,1)S(1)}, u32[]{:S(2)}, u32[]{:S(2)}) %collective-permute-start.14) | collective-permute-done | bytes 524320 | tf_op jit(solution)/shard_map/ppermute | solution.py:45
  176.7 26.1 %mlp_block.1 = (bf16[768,2048]{1,0:T(8,128)(2,1)}, bf16[1024,768]{1,0:T(8,128)(2,1)}, bf16[1024,1536]{1,0:T(8,128)(2,1)}, bf16[512,2048]{1,0:T(8,128)(2,1)}, bf16[512,2048]{1,0:T(8,128)(2,1)}) custom-call(bf16[128,2048]{1,0:T(8,128)(2,1)} %copy-done.22, bf16[128,2048]{1,0:T(8,128)(2,1)} %copy-done.48, bf16[128,2048]{1,0:T(8,128)(2,1)} %copy-done.47, ...), custom_call_target="tpu_custom_call" | custom-call | flops 16106127360 | bytes 29884416 | tf_op jit(solution)/shard_map/mlp_block/pallas_call | solution.py:192
  203.0 4.3 collective-permute-done.27.refs_1_
  210.7 2.0 collective-permute-start.30
  212.7 18.5 %mlp_weight_grads.1 = (bf16[16,576,512]{2,1,0:T(8,128)(2,1)}, f32[8,128]{1,0:T(8,128)}) custom-call(bf16[128,2048]{1,0:T(8,128)(2,1)} %copy-done.22, bf16[128,2048]{1,0:T(8,128)(2,1)} %copy-done.48, bf16[128,2048]{1,0:T(8,128)(2,1)} %copy-done.47, bf16[128,2048]{1,0:T(8,128)(2,1)} %copy-done.46, bf16[128,2048]{1,0:T(8,128)(2,1)} %copy-done.50, ...), custom_call_target="tpu_custom_call" | custom-call | flops 9663676416 | bytes 22548480 | tf_op jit(solution)/shard_map/mlp_weight_grads/pallas_call | solution.py:192
  231.3 3.2 collective-permute-done.29.refs_2_
  244.1 7.1 %mlp_out.1 = (bf16[512,2048]{1,0:T(8,128)(2,1)}, bf16[512,2048]{1,0:T(8,128)(2,1)}) custom-call(bf16[1024,768]{1,0:T(8,128)(2,1)} %get-tuple-element.121.refs_17_.refs_0_, bf16[768,2048]{1,0:T(8,128)(2,1)} %get-tuple-element.122.refs_1_, bf16[128,2048]{1,0:T(8,128)(2,1)} %get-tuple-element.132.refs_2_.refs_0_.refs_1_), custom_call_target="tpu_custom_call" | custom-call | flops 3221225472 | bytes 8912896 | tf_op jit(solution)/shard_map/mlp_out/pallas_call | solution.py:192
  251.2 4.1 collective-permute-done.33.refs_3_
  255.3 12.4 %collective-permute-done.32.refs_2_ = bf16[128,2048]{1,0:T(8,128)(2,1)S(1)} collective-permute-done((bf16[128,2048]{1,0:T(8,128)(2,1)}, bf16[128,2048]{1,0:T(8,128)(2,1)S(1)}, u32[]{:S(2)}, u32[]{:S(2)}) %collective-permute-start.32) | collective-permute-done | bytes 524320 | tf_op jit(solution)/shard_map/ppermute | solution.py:45
  269.6 3.7 collective-permute-done.38.refs_4_
  276.7 5.8 %out_weight_grads.1 = bf16[256,2048]{1,0:T(8,128)(2,1)} custom-call(bf16[128,2048]{1,0:T(8,128)(2,1)} %get-tuple-element.132.refs_2_.refs_0_.refs_1_, bf16[128,2048]{1,0:T(8,128)(2,1)} %get-tuple-element.140.refs_1_, bf16[128,2048]{1,0:T(8,128)(2,1)} %get-tuple-element.141.refs_2_, bf16[128,2048]{1,0:T(8,128)(2,1)} %get-tuple-element.142.refs_3_, ...), custom_call_target="tpu_custom_call" | custom-call | flops 1073741824 | bytes 5767168 | tf_op jit(solution)/shard_map/out_weight_grads/pallas_call | solution.py:192
  282.5 5.9 %all-to-all-start.1 = ((bf16[16,16,2048]{2,1,0:T(8,128)(2,1)}), bf16[16,16,2048]{2,1,0:T(8,128)(2,1)S(1)}, u32[]{:S(2)}, u32[]{:S(2)}) async-start(bf16[16,16,2048]{2,1,0:T(8,128)(2,1)} %bitcast.26), calls=%async_computation.1 | async-start | bytes 2097152 | tf_op jit(solution)/shard_map/all_to_all | solution.py:950
  290.1 2.8 output_add.1
  294.8 2.4 collective-permute-start.37
  297.2 21.8 %head_back.1 = (bf16[512,2048]{1,0:T(8,128)(2,1)}, bf16[512,2048]{1,0:T(8,128)(2,1)}, bf16[128,16,640]{2,1,0:T(8,128)(2,1)}, f32[8,128]{1,0:T(8,128)}) custom-call(bf16[128,2048]{1,0:T(8,128)(2,1)} %get-tuple-element.132.refs_2_.refs_0_.refs_1_, bf16[128,2048]{1,0:T(8,128)(2,1)} %get-tuple-element.140.refs_1_, bf16[128,2048]{1,0:T(8,128)(2,1)} %get-tuple-element.141.refs_2_, ...), custom_call_target="tpu_custom_call" | custom-call | tf_op jit(solution)/shard_map/head_back/pallas_call | solution.py:192
  321.8 2.6 output_end.1.refs_2_
  324.4 9.8 %all-to-all-start.2 = ((bf16[128,16,640]{2,1,0:T(8,128)(2,1)}), bf16[128,16,640]{2,1,0:T(8,128)(2,1)}, u32[]{:S(2)}, u32[]{:S(2)}) async-start(bf16[128,16,640]{2,1,0:T(8,128)(2,1)} %get-tuple-element.164), calls=%async_computation.2 | async-start | bytes 5242880 | tf_op jit(solution)/shard_map/all_to_all | solution.py:978
  334.4 4.2 collective-permute-done.42.refs_1_
  344.6 18.8 %reduce-scatter.2.cloned.1.call-done.refs_0_ = bf16[576,512]{1,0:T(8,128)(2,1)} async-done(((bf16[9216,512]{1,0:T(8,128)(2,1)}), bf16[576,512]{1,0:T(8,128)(2,1)}) %reduce-scatter.2.cloned.1.call-update) | async-done | bytes 589840 | tf_op jit(solution)/shard_map/reduce_scatter | solution.py:923
  363.3 1.8 slice.41
  365.1 3.4 all-to-all-done.2.refs_11_.refs_0_
  368.5 5.8 %all-to-all-start.3 = ((bf16[8,48,512]{2,1,0:T(8,128)(2,1)}), bf16[8,48,512]{2,1,0:T(8,128)(2,1)}, u32[]{:S(2)}, u32[]{:S(2)}) async-start(bf16[8,48,512]{2,1,0:T(8,128)(2,1)} %bitcast.27), calls=%async_computation.4 | async-start | bytes 786432 | tf_op jit(solution)/shard_map/all_to_all | solution.py:987
  375.2 3.0 collective-permute-start.47
  378.2 4.6 %collective-permute-start.46 = (bf16[16,2048]{1,0:T(8,128)(2,1)S(1)}, bf16[16,2048]{1,0:T(8,128)(2,1)S(1)}, u32[]{:S(2)}, u32[]{:S(2)}) collective-permute-start(bf16[16,2048]{1,0:T(8,128)(2,1)S(1)} %copy-done.16), channel_id=1, source_target_pairs={{0,0},{4,1},{8,2},{12,3},{32,4},{36,5},{40,6},{44,7},{64,8},{68,9}... | collective-permute-start | bytes 196616 | tf_op jit(solution)/shard_map/ppermute | solution.py:989
  382.8 3.9 collective-permute-done.43.refs_1_
  386.8 3.1 input_end.1
  390.5 17.3 %collective-permute-done.47.refs_1_ = bf16[192,512]{1,0:T(8,128)(2,1)S(1)} collective-permute-done((bf16[192,512]{1,0:T(8,128)(2,1)S(1)}, bf16[192,512]{1,0:T(8,128)(2,1)S(1)}, u32[]{:S(2)}, u32[]{:S(2)}) %collective-permute-start.47) | collective-permute-done | bytes 196640 | tf_op jit(solution)/shard_map/ppermute | solution.py:988
  408.5 5.3 %mlp_update.1 = (f32[16,6144]{1,0:T(8,128)}, f32[16,6144]{1,0:T(8,128)}, f32[16,6144]{1,0:T(8,128)}, f32[16,6144]{1,0:T(8,128)}, f32[16,6144]{1,0:T(8,128)}, /*i...) custom-call(bf16[8,48,512]{2,1,0:T(8,128)(2,1)} %all-to-all-done.3.refs, ...), custom_call_target="tpu_custom_call" | custom-call | bytes 7671808 | tf_op jit(solution)/shard_map/mlp_update/pallas_call | solution.py:192
  414.4 5.1 %head_update.1 = (f32[16,2048]{1,0:T(8,128)}, f32[16,2048]{1,0:T(8,128)}, f32[16,2048]{1,0:T(8,128)}, f32[16,1024]{1,0:T(8,128)}, f32[16,1024]{1,0:T(8,128)}, /*...) custom-call(bf16[128,16,640]{2,1,0:T(8,128)(2,1)} %all-to-all-done.2, ...), custom_call_target="tpu_custom_call" | custom-call | bytes 5047088 | tf_op jit(solution)/shard_map/head_update/pallas_call | solution.py:192
  (241 shorter events, 58.9 us)
Async XLA Ops:
  10.4 28.2 %all-to-all-start = ((bf16[8,80,512]{2,1,0:T(8,128)(2,1)}), bf16[8,80,512]{2,1,0:T(8,128)(2,1)S(1)}, u32[]{:S(2)}, u32[]{:S(2)}) async-start(bf16[8,80,512]{2,1,0:T(8,128)(2,1)} %get-tuple-element.110), calls=%async_computation | async-start | bytes 1310720 | tf_op jit(solution)/shard_map/all_to_all | solution.py:800
  15.3 82.1 %all-gather.5.cloned.1.call-start = ((), (), s32[]{:S(2)}) async-start(), calls=%async_computation.6 | async-start | bytes 3620864 | tf_op jit(solution)/shard_map/all_gather | solution.py:815
  15.3 23.3 %collective-permute-start.7 = (bf16[256,512]{1,0:T(8,128)(2,1)}, bf16[256,512]{1,0:T(8,128)(2,1)S(1)}, u32[]{:S(2)}, u32[]{:S(2)}) collective-permute-start(bf16[256,512]{1,0:T(8,128)(2,1)} %get-tuple-element.111), channel_id=1, source_target_pairs={{0,0},{1,4},{2,8},{3,12},{4,32},{5,36},{6,40},{7,44},{8,64},{9,68}... | collective-permute-start | bytes 786440 | tf_op jit(solution)/shard_map/ppermute | solution.py:801
  20.6 9.5 %collective-permute-start.8 = (s32[10]{0:T(128)}, s32[10]{0:T(128)S(1)}, u32[]{:S(2)}, u32[]{:S(2)}) collective-permute-start(s32[10]{0:T(128)} %table_then.1), channel_id=1, source_target_pairs={{0,16},{16,0},{1,17},{17,1},{2,18},{18,2},{3,19},{19,3},{4,20},{20... | collective-permute-start | bytes 128 | tf_op jit(solution)/shard_map/ppermute | solution.py:796
  40.2 136.5 %all-gather.7.cloned.1.call-start = ((), (), s32[]{:S(2)}) async-start(), calls=%async_computation.7 | async-start | bytes 10027008 | tf_op jit(solution)/shard_map/all_gather | solution.py:830
  41.1 29.3 %collective-permute-start.3 = (bf16[128,2048]{1,0:T(8,128)(2,1)}, bf16[128,2048]{1,0:T(8,128)(2,1)}, u32[]{:S(2)}, u32[]{:S(2)}) collective-permute-start(bf16[128,2048]{1,0:T(8,128)(2,1)} %tokens_then.1.refs_0_), channel_id=1, source_target_pairs={{0,1},{1,0},{2,3},{3,2},{4,5},{5,4},{6,7},{7,6},{8,9},{9,8},{10,11... | collective-permute-start | bytes 1572872 | tf_op jit(solution)/shard_map/ppermute | solution.py:49
  41.1 15.0 %collective-permute-start.2 = (bf16[128,2048]{1,0:T(8,128)(2,1)}, bf16[128,2048]{1,0:T(8,128)(2,1)}, u32[]{:S(2)}, u32[]{:S(2)}) collective-permute-start(bf16[128,2048]{1,0:T(8,128)(2,1)} %tokens_then.1.refs_0_), channel_id=1, source_target_pairs={{18,0},{0,16},{16,2},{2,18},{19,1},{1,17},{17,3},{3,19},{22,4},{4,... | collective-permute-start | bytes 1572872 | tf_op jit(solution)/shard_map/ppermute | solution.py:45
  41.1 31.8 %collective-permute-start.1 = (bf16[128,2048]{1,0:T(8,128)(2,1)}, bf16[128,2048]{1,0:T(8,128)(2,1)}, u32[]{:S(2)}, u32[]{:S(2)}) collective-permute-start(bf16[128,2048]{1,0:T(8,128)(2,1)} %tokens_then.1.refs_0_), channel_id=1, source_target_pairs={{16,0},{2,16},{18,2},{0,18},{17,1},{3,17},{19,3},{1,19},{20,4},{6,... | collective-permute-start | bytes 1572872 | tf_op jit(solution)/shard_map/ppermute | solution.py:45
  43.1 23.1 %collective-permute-start = (bf16[128,2048]{1,0:T(8,128)(2,1)}, bf16[128,2048]{1,0:T(8,128)(2,1)S(1)}, u32[]{:S(2)}, u32[]{:S(2)}) collective-permute-start(bf16[128,2048]{1,0:T(8,128)(2,1)} %tokens_then.1.refs_0_), channel_id=1, source_target_pairs={{2,0},{18,16},{0,2},{16,18},{3,1},{19,17},{1,3},{17,19},{6,4},{22,... | collective-permute-start | bytes 1572872 | tf_op jit(solution)/shard_map/ppermute | solution.py:45
  56.1 16.8 %collective-permute-start.6 = (bf16[128,2048]{1,0:T(8,128)(2,1)}, bf16[128,2048]{1,0:T(8,128)(2,1)S(1)}, u32[]{:S(2)}, u32[]{:S(2)}) collective-permute-start(bf16[128,2048]{1,0:T(8,128)(2,1)} %collective-permute-done.2.refs_3_), channel_id=1, source_target_pairs={{0,1},{1,0},{2,3},{3,2},{4,5},{5,4},{6,7},{7,6},{8,9},{9,8},{10,11... | collective-permute-start | bytes 1572872 | tf_op jit(solution)/shard_map/ppermute | solution.py:49
  67.0 25.9 %collective-permute-start.22 = (bf16[128,2048]{1,0:T(8,128)(2,1)}, bf16[128,2048]{1,0:T(8,128)(2,1)S(1)}, u32[]{:S(2)}, u32[]{:S(2)}) collective-permute-start(bf16[128,2048]{1,0:T(8,128)(2,1)} %cotangent_then.1.refs_8_), channel_id=1, source_target_pairs={{18,0},{0,16},{16,2},{2,18},{19,1},{1,17},{17,3},{3,19},{22,4},{4,... | collective-permute-start | bytes 1572872 | tf_op jit(solution)/shard_map/ppermute | solution.py:45
  70.3 25.9 %collective-permute-start.21 = (bf16[128,2048]{1,0:T(8,128)(2,1)}, bf16[128,2048]{1,0:T(8,128)(2,1)S(1)}, u32[]{:S(2)}, u32[]{:S(2)}) collective-permute-start(bf16[128,2048]{1,0:T(8,128)(2,1)} %cotangent_then.1.refs_8_), channel_id=1, source_target_pairs={{16,0},{2,16},{18,2},{0,18},{17,1},{3,17},{19,3},{1,19},{20,4},{6,... | collective-permute-start | bytes 1572872 | tf_op jit(solution)/shard_map/ppermute | solution.py:45
  70.3 25.9 %collective-permute-start.20 = (bf16[128,2048]{1,0:T(8,128)(2,1)}, bf16[128,2048]{1,0:T(8,128)(2,1)}, u32[]{:S(2)}, u32[]{:S(2)}) collective-permute-start(bf16[128,2048]{1,0:T(8,128)(2,1)} %cotangent_then.1.refs_8_), channel_id=1, source_target_pairs={{2,0},{18,16},{0,2},{16,18},{3,1},{19,17},{1,3},{17,19},{6,4},{22,... | collective-permute-start | bytes 1572872 | tf_op jit(solution)/shard_map/ppermute | solution.py:45
  72.9 23.3 %collective-permute-start.4 = (bf16[128,2048]{1,0:T(8,128)(2,1)}, bf16[128,2048]{1,0:T(8,128)(2,1)}, u32[]{:S(2)}, u32[]{:S(2)}) collective-permute-start(bf16[128,2048]{1,0:T(8,128)(2,1)} %copy-done.28), channel_id=1, source_target_pairs={{0,1},{1,0},{2,3},{3,2},{4,5},{5,4},{6,7},{7,6},{8,9},{9,8},{10,11... | collective-permute-start | bytes 1572872 | tf_op jit(solution)/shard_map/ppermute | solution.py:49
  73.8 5.3 %collective-permute-start.5 = (bf16[128,2048]{1,0:T(8,128)(2,1)}, bf16[128,2048]{1,0:T(8,128)(2,1)S(1)}, u32[]{:S(2)}, u32[]{:S(2)}) collective-permute-start(bf16[128,2048]{1,0:T(8,128)(2,1)} %collective-permute-done.1.refs_2_), channel_id=1, source_target_pairs={{0,1},{1,0},{2,3},{3,2},{4,5},{5,4},{6,7},{7,6},{8,9},{9,8},{10,11... | collective-permute-start | bytes 1572872 | tf_op jit(solution)/shard_map/ppermute | solution.py:49
  97.1 266.2 %reduce-scatter.2.cloned.1.call-start = ((), (), s32[]{:S(2)}) async-start(), calls=%async_computation.5 | async-start | bytes 10027008 | tf_op jit(solution)/shard_map/reduce_scatter | solution.py:923
  120.0 16.4 %collective-permute-start.10 = (bf16[128,2048]{1,0:T(8,128)(2,1)S(1)}, bf16[128,2048]{1,0:T(8,128)(2,1)S(1)}, u32[]{:S(2)}, u32[]{:S(2)}) collective-permute-start(bf16[128,2048]{1,0:T(8,128)(2,1)S(1)} %get-tuple-element.116), channel_id=1, source_target_pairs={{2,0},{18,16},{0,2},{16,18},{3,1},{19,17},{1,3},{17,19},{6,4},{22,... | collective-permute-start | bytes 1572872 | tf_op jit(solution)/shard_map/ppermute | solution.py:45
  120.1 24.5 %collective-permute-start.11 = (bf16[128,2048]{1,0:T(8,128)(2,1)S(1)}, bf16[128,2048]{1,0:T(8,128)(2,1)S(1)}, u32[]{:S(2)}, u32[]{:S(2)}) collective-permute-start(bf16[128,2048]{1,0:T(8,128)(2,1)S(1)} %get-tuple-element.117), channel_id=1, source_target_pairs={{18,0},{0,16},{16,2},{2,18},{19,1},{1,17},{17,3},{3,19},{22,4},{4,... | collective-permute-start | bytes 1572872 | tf_op jit(solution)/shard_map/ppermute | solution.py:45
  120.9 25.9 %collective-permute-start.12 = (bf16[128,2048]{1,0:T(8,128)(2,1)S(1)}, bf16[128,2048]{1,0:T(8,128)(2,1)S(1)}, u32[]{:S(2)}, u32[]{:S(2)}) collective-permute-start(bf16[128,2048]{1,0:T(8,128)(2,1)S(1)} %get-tuple-element.118), channel_id=1, source_target_pairs={{16,0},{2,16},{18,2},{0,18},{17,1},{3,17},{19,3},{1,19},{20,4},{6,... | collective-permute-start | bytes 1572872 | tf_op jit(solution)/shard_map/ppermute | solution.py:45
  122.2 27.3 %collective-permute-start.23 = (bf16[128,2048]{1,0:T(8,128)(2,1)S(1)}, bf16[128,2048]{1,0:T(8,128)(2,1)S(1)}, u32[]{:S(2)}, u32[]{:S(2)}) collective-permute-start(bf16[128,2048]{1,0:T(8,128)(2,1)S(1)} %copy-done.29), channel_id=1, source_target_pairs={{0,1},{1,0},{2,3},{3,2},{4,5},{5,4},{6,7},{7,6},{8,9},{9,8},{10,11... | collective-permute-start | bytes 1572872 | tf_op jit(solution)/shard_map/ppermute | solution.py:49
  122.2 27.6 %collective-permute-start.26 = (bf16[128,2048]{1,0:T(8,128)(2,1)S(1)}, bf16[128,2048]{1,0:T(8,128)(2,1)S(1)}, u32[]{:S(2)}, u32[]{:S(2)}) collective-permute-start(bf16[128,2048]{1,0:T(8,128)(2,1)S(1)} %copy-done.35), channel_id=1, source_target_pairs={{0,1},{1,0},{2,3},{3,2},{4,5},{5,4},{6,7},{7,6},{8,9},{9,8},{10,11... | collective-permute-start | bytes 1572872 | tf_op jit(solution)/shard_map/ppermute | solution.py:49
  136.4 13.4 %collective-permute-start.25 = (bf16[128,2048]{1,0:T(8,128)(2,1)S(1)}, bf16[128,2048]{1,0:T(8,128)(2,1)S(1)}, u32[]{:S(2)}, u32[]{:S(2)}) collective-permute-start(bf16[128,2048]{1,0:T(8,128)(2,1)S(1)} %copy-done.37), channel_id=1, source_target_pairs={{0,1},{1,0},{2,3},{3,2},{4,5},{5,4},{6,7},{7,6},{8,9},{9,8},{10,11... | collective-permute-start | bytes 1572872 | tf_op jit(solution)/shard_map/ppermute | solution.py:49
  147.4 14.8 %collective-permute-start.15 = (bf16[128,2048]{1,0:T(8,128)(2,1)S(1)}, bf16[128,2048]{1,0:T(8,128)(2,1)S(1)}, u32[]{:S(2)}, u32[]{:S(2)}) collective-permute-start(bf16[128,2048]{1,0:T(8,128)(2,1)S(1)} %get-tuple-element.119.refs_0_), channel_id=1, source_target_pairs={{18,0},{0,16},{16,2},{2,18},{19,1},{1,17},{17,3},{3,19},{22,4},{4,... | collective-permute-start | bytes 1572872 | tf_op jit(solution)/shard_map/ppermute | solution.py:45
  148.0 25.9 %collective-permute-start.14 = (bf16[128,2048]{1,0:T(8,128)(2,1)S(1)}, bf16[128,2048]{1,0:T(8,128)(2,1)S(1)}, u32[]{:S(2)}, u32[]{:S(2)}) collective-permute-start(bf16[128,2048]{1,0:T(8,128)(2,1)S(1)} %get-tuple-element.119.refs_0_), channel_id=1, source_target_pairs={{16,0},{2,16},{18,2},{0,18},{17,1},{3,17},{19,3},{1,19},{20,4},{6,... | collective-permute-start | bytes 1572872 | tf_op jit(solution)/shard_map/ppermute | solution.py:45
  149.5 24.5 %collective-permute-start.13 = (bf16[128,2048]{1,0:T(8,128)(2,1)S(1)}, bf16[128,2048]{1,0:T(8,128)(2,1)S(1)}, u32[]{:S(2)}, u32[]{:S(2)}) collective-permute-start(bf16[128,2048]{1,0:T(8,128)(2,1)S(1)} %get-tuple-element.119.refs_0_), channel_id=1, source_target_pairs={{2,0},{18,16},{0,2},{16,18},{3,1},{19,17},{1,3},{17,19},{6,4},{22,... | collective-permute-start | bytes 1572872 | tf_op jit(solution)/shard_map/ppermute | solution.py:45
  149.8 24.7 %collective-permute-start.24 = (bf16[128,2048]{1,0:T(8,128)(2,1)}, bf16[128,2048]{1,0:T(8,128)(2,1)S(1)}, u32[]{:S(2)}, u32[]{:S(2)}) collective-permute-start(bf16[128,2048]{1,0:T(8,128)(2,1)} %collective-permute-done.20.refs_8_.refs_9_), channel_id=1, source_target_pairs={{0,1},{1,0},{2,3},{3,2},{4,5},{5,4},{6,7},{7,6},{8,9},{9,8},{10,11... | collective-permute-start | bytes 1572872 | tf_op jit(solution)/shard_map/ppermute | solution.py:49
  149.8 24.7 %collective-permute-start.16 = (bf16[128,2048]{1,0:T(8,128)(2,1)S(1)}, bf16[128,2048]{1,0:T(8,128)(2,1)S(1)}, u32[]{:S(2)}, u32[]{:S(2)}) collective-permute-start(bf16[128,2048]{1,0:T(8,128)(2,1)S(1)} %get-tuple-element.119.refs_0_), channel_id=1, source_target_pairs={{0,1},{1,0},{2,3},{3,2},{4,5},{5,4},{6,7},{7,6},{8,9},{9,8},{10,11... | collective-permute-start | bytes 1572872 | tf_op jit(solution)/shard_map/ppermute | solution.py:49
  162.2 12.3 %collective-permute-start.19 = (bf16[128,2048]{1,0:T(8,128)(2,1)S(1)}, bf16[128,2048]{1,0:T(8,128)(2,1)S(1)}, u32[]{:S(2)}, u32[]{:S(2)}) collective-permute-start(bf16[128,2048]{1,0:T(8,128)(2,1)S(1)} %collective-permute-done.15.refs_3_), channel_id=1, source_target_pairs={{0,1},{1,0},{2,3},{3,2},{4,5},{5,4},{6,7},{7,6},{8,9},{9,8},{10,11... | collective-permute-start | bytes 1572872 | tf_op jit(solution)/shard_map/ppermute | solution.py:49
  209.4 21.9 %collective-permute-start.28 = (bf16[128,2048]{1,0:T(8,128)(2,1)S(1)}, bf16[128,2048]{1,0:T(8,128)(2,1)S(1)}, u32[]{:S(2)}, u32[]{:S(2)}) collective-permute-start(bf16[128,2048]{1,0:T(8,128)(2,1)S(1)} %get-tuple-element.126.refs_18_), channel_id=1, source_target_pairs={{2,0},{18,16},{0,2},{16,18},{3,1},{19,17},{1,3},{17,19},{6,4},{22,... | collective-permute-start | bytes 1572872 | tf_op jit(solution)/shard_map/ppermute | solution.py:45
  210.7 23.7 %collective-permute-start.29 = (bf16[128,2048]{1,0:T(8,128)(2,1)S(1)}, bf16[128,2048]{1,0:T(8,128)(2,1)S(1)}, u32[]{:S(2)}, u32[]{:S(2)}) collective-permute-start(bf16[128,2048]{1,0:T(8,128)(2,1)S(1)} %get-tuple-element.127.refs_19_), channel_id=1, source_target_pairs={{18,0},{0,16},{16,2},{2,18},{19,1},{1,17},{17,3},{3,19},{22,4},{4,... | collective-permute-start | bytes 1572872 | tf_op jit(solution)/shard_map/ppermute | solution.py:45
  210.7 25.4 %collective-permute-start.30 = (bf16[128,2048]{1,0:T(8,128)(2,1)S(1)}, bf16[128,2048]{1,0:T(8,128)(2,1)S(1)}, u32[]{:S(2)}, u32[]{:S(2)}) collective-permute-start(bf16[128,2048]{1,0:T(8,128)(2,1)S(1)} %get-tuple-element.128.refs_20_), channel_id=1, source_target_pairs={{16,0},{2,16},{18,2},{0,18},{17,1},{3,17},{19,3},{1,19},{20,4},{6,... | collective-permute-start | bytes 1572872 | tf_op jit(solution)/shard_map/ppermute | solution.py:45
  240.3 15.1 %collective-permute-start.33 = (bf16[128,2048]{1,0:T(8,128)(2,1)}, bf16[128,2048]{1,0:T(8,128)(2,1)S(1)}, u32[]{:S(2)}, u32[]{:S(2)}) collective-permute-start(bf16[128,2048]{1,0:T(8,128)(2,1)} %get-tuple-element.132.refs_2_.refs_0_.refs_1_), channel_id=1, source_target_pairs={{18,0},{0,16},{16,2},{2,18},{19,1},{1,17},{17,3},{3,19},{22,4},{4,... | collective-permute-start | bytes 1572872 | tf_op jit(solution)/shard_map/ppermute | solution.py:45
  241.3 26.5 %collective-permute-start.32 = (bf16[128,2048]{1,0:T(8,128)(2,1)}, bf16[128,2048]{1,0:T(8,128)(2,1)S(1)}, u32[]{:S(2)}, u32[]{:S(2)}) collective-permute-start(bf16[128,2048]{1,0:T(8,128)(2,1)} %get-tuple-element.132.refs_2_.refs_0_.refs_1_), channel_id=1, source_target_pairs={{16,0},{2,16},{18,2},{0,18},{17,1},{3,17},{19,3},{1,19},{20,4},{6,... | collective-permute-start | bytes 1572872 | tf_op jit(solution)/shard_map/ppermute | solution.py:45
  242.6 25.2 %collective-permute-start.31 = (bf16[128,2048]{1,0:T(8,128)(2,1)}, bf16[128,2048]{1,0:T(8,128)(2,1)}, u32[]{:S(2)}, u32[]{:S(2)}) collective-permute-start(bf16[128,2048]{1,0:T(8,128)(2,1)} %get-tuple-element.132.refs_2_.refs_0_.refs_1_), channel_id=1, source_target_pairs={{2,0},{18,16},{0,2},{16,18},{3,1},{19,17},{1,3},{17,19},{6,4},{22,... | collective-permute-start | bytes 1572872 | tf_op jit(solution)/shard_map/ppermute | solution.py:45
  268.5 19.9 %collective-permute-start.34 = (bf16[512,2048]{1,0:T(8,128)(2,1)}, bf16[512,2048]{1,0:T(8,128)(2,1)}, u32[]{:S(2)}, u32[]{:S(2)}) collective-permute-start(bf16[512,2048]{1,0:T(8,128)(2,1)} %get-tuple-element.135), channel_id=1, source_target_pairs={{0,1},{1,0},{2,3},{3,2},{4,5},{5,4},{6,7},{7,6},{8,9},{9,8},{10,11... | collective-permute-start | bytes 6291464 | tf_op jit(solution)/shard_map/ppermute | solution.py:49
  269.0 5.7 %collective-permute-start.40 = (bf16[128,2048]{1,0:T(8,128)(2,1)}, bf16[128,2048]{1,0:T(8,128)(2,1)S(1)}, u32[]{:S(2)}, u32[]{:S(2)}) collective-permute-start(bf16[128,2048]{1,0:T(8,128)(2,1)} %get-tuple-element.141.refs_2_), channel_id=1, source_target_pairs={{0,1},{1,0},{2,3},{3,2},{4,5},{5,4},{6,7},{7,6},{8,9},{9,8},{10,11... | collective-permute-start | bytes 1572872 | tf_op jit(solution)/shard_map/ppermute | solution.py:49
  269.6 6.3 %collective-permute-start.41 = (bf16[128,2048]{1,0:T(8,128)(2,1)}, bf16[128,2048]{1,0:T(8,128)(2,1)S(1)}, u32[]{:S(2)}, u32[]{:S(2)}) collective-permute-start(bf16[128,2048]{1,0:T(8,128)(2,1)} %get-tuple-element.142.refs_3_), channel_id=1, source_target_pairs={{0,1},{1,0},{2,3},{3,2},{4,5},{5,4},{6,7},{7,6},{8,9},{9,8},{10,11... | collective-permute-start | bytes 1572872 | tf_op jit(solution)/shard_map/ppermute | solution.py:49
  282.5 36.5 %all-to-all-start.1 = ((bf16[16,16,2048]{2,1,0:T(8,128)(2,1)}), bf16[16,16,2048]{2,1,0:T(8,128)(2,1)S(1)}, u32[]{:S(2)}, u32[]{:S(2)}) async-start(bf16[16,16,2048]{2,1,0:T(8,128)(2,1)} %bitcast.26), calls=%async_computation.1 | async-start | bytes 2097152 | tf_op jit(solution)/shard_map/all_to_all | solution.py:950
  293.9 26.6 %collective-permute-start.35 = (bf16[128,2048]{1,0:T(8,128)(2,1)}, bf16[128,2048]{1,0:T(8,128)(2,1)}, u32[]{:S(2)}, u32[]{:S(2)}) collective-permute-start(bf16[128,2048]{1,0:T(8,128)(2,1)} %get-tuple-element.137.refs_24_), channel_id=1, source_target_pairs={{2,0},{18,16},{0,2},{16,18},{3,1},{19,17},{1,3},{17,19},{6,4},{22,... | collective-permute-start | bytes 1572872 | tf_op jit(solution)/shard_map/ppermute | solution.py:45
  294.8 25.7 %collective-permute-start.36 = (bf16[128,2048]{1,0:T(8,128)(2,1)}, bf16[128,2048]{1,0:T(8,128)(2,1)}, u32[]{:S(2)}, u32[]{:S(2)}) collective-permute-start(bf16[128,2048]{1,0:T(8,128)(2,1)} %get-tuple-element.138.refs_25_), channel_id=1, source_target_pairs={{18,0},{0,16},{16,2},{2,18},{19,1},{1,17},{17,3},{3,19},{22,4},{4,... | collective-permute-start | bytes 1572872 | tf_op jit(solution)/shard_map/ppermute | solution.py:45
  294.8 25.8 %collective-permute-start.37 = (bf16[128,2048]{1,0:T(8,128)(2,1)S(1)}, bf16[128,2048]{1,0:T(8,128)(2,1)}, u32[]{:S(2)}, u32[]{:S(2)}) collective-permute-start(bf16[128,2048]{1,0:T(8,128)(2,1)S(1)} %get-tuple-element.139.refs_26_), channel_id=1, source_target_pairs={{16,0},{2,16},{18,2},{0,18},{17,1},{3,17},{19,3},{1,19},{20,4},{6,... | collective-permute-start | bytes 1572872 | tf_op jit(solution)/shard_map/ppermute | solution.py:45
  324.4 44.1 %all-to-all-start.2 = ((bf16[128,16,640]{2,1,0:T(8,128)(2,1)}), bf16[128,16,640]{2,1,0:T(8,128)(2,1)}, u32[]{:S(2)}, u32[]{:S(2)}) async-start(bf16[128,16,640]{2,1,0:T(8,128)(2,1)} %get-tuple-element.164), calls=%async_computation.2 | async-start | bytes 5242880 | tf_op jit(solution)/shard_map/all_to_all | solution.py:978
  341.0 41.8 %collective-permute-start.44 = (bf16[128,2048]{1,0:T(8,128)(2,1)}, bf16[128,2048]{1,0:T(8,128)(2,1)}, u32[]{:S(2)}, u32[]{:S(2)}) collective-permute-start(bf16[128,2048]{1,0:T(8,128)(2,1)} %get-tuple-element.160), channel_id=1, source_target_pairs={{18,0},{0,16},{16,2},{2,18},{19,1},{1,17},{17,3},{3,19},{22,4},{4,... | collective-permute-start | bytes 1572872 | tf_op jit(solution)/shard_map/ppermute | solution.py:45
  342.2 40.6 %collective-permute-start.45 = (bf16[128,2048]{1,0:T(8,128)(2,1)}, bf16[128,2048]{1,0:T(8,128)(2,1)}, u32[]{:S(2)}, u32[]{:S(2)}) collective-permute-start(bf16[128,2048]{1,0:T(8,128)(2,1)} %get-tuple-element.161), channel_id=1, source_target_pairs={{16,0},{2,16},{18,2},{0,18},{17,1},{3,17},{19,3},{1,19},{20,4},{6,... | collective-permute-start | bytes 1572872 | tf_op jit(solution)/shard_map/ppermute | solution.py:45
  343.1 43.6 %collective-permute-start.43 = (bf16[128,2048]{1,0:T(8,128)(2,1)S(1)}, bf16[128,2048]{1,0:T(8,128)(2,1)}, u32[]{:S(2)}, u32[]{:S(2)}) collective-permute-start(bf16[128,2048]{1,0:T(8,128)(2,1)S(1)} %get-tuple-element.159.refs_1_), channel_id=1, source_target_pairs={{2,0},{18,16},{0,2},{16,18},{3,1},{19,17},{1,3},{17,19},{6,4},{22,... | collective-permute-start | bytes 1572872 | tf_op jit(solution)/shard_map/ppermute | solution.py:45
  368.5 39.3 %all-to-all-start.3 = ((bf16[8,48,512]{2,1,0:T(8,128)(2,1)}), bf16[8,48,512]{2,1,0:T(8,128)(2,1)}, u32[]{:S(2)}, u32[]{:S(2)}) async-start(bf16[8,48,512]{2,1,0:T(8,128)(2,1)} %bitcast.27), calls=%async_computation.4 | async-start | bytes 786432 | tf_op jit(solution)/shard_map/all_to_all | solution.py:987
  375.2 32.6 %collective-permute-start.47 = (bf16[192,512]{1,0:T(8,128)(2,1)S(1)}, bf16[192,512]{1,0:T(8,128)(2,1)S(1)}, u32[]{:S(2)}, u32[]{:S(2)}) collective-permute-start(bf16[192,512]{1,0:T(8,128)(2,1)S(1)} %slice.42), channel_id=1, source_target_pairs={{0,0},{4,1},{8,2},{12,3},{32,4},{36,5},{40,6},{44,7},{64,8},{68,9}... | collective-permute-start | bytes 589832 | tf_op jit(solution)/shard_map/ppermute | solution.py:988
  378.2 35.6 %collective-permute-start.46 = (bf16[16,2048]{1,0:T(8,128)(2,1)S(1)}, bf16[16,2048]{1,0:T(8,128)(2,1)S(1)}, u32[]{:S(2)}, u32[]{:S(2)}) collective-permute-start(bf16[16,2048]{1,0:T(8,128)(2,1)S(1)} %copy-done.16), channel_id=1, source_target_pairs={{0,0},{4,1},{8,2},{12,3},{32,4},{36,5},{40,6},{44,7},{64,8},{68,9}... | collective-permute-start | bytes 196616 | tf_op jit(solution)/shard_map/ppermute | solution.py:989
  (62 other events, 575.5 us)
Sparse Core Ops, SparseCore 0:
  40.4 49.0 all-gather.4
  97.2 75.7 all-gather.6
  240.4 122.8 reduce-scatter.1
where the time goes:
time: 433 us; the launch traced here: 426 us
  waiting for transfers between devices  189 us (44%)
  Pallas kernels  121 us (28%)
  starting transfers between devices  69.6 us (16%)
  local copies, waits for them, and re-layouts  25.6 us (6%)
  between operations  14.6 us (3%)
  other arithmetic  6.77 us (2%)
    pallas_call x19, Pallas kernels, call(): pl.pallas_call(run, out_shape=tuple(outs), in_specs=in_specs + after_spec...  121 us
    ppermute x24, waiting for transfers between devices, from_chip(): return lax.ppermute(value, CHIPS, pairs)  111 us
    ppermute x24, starting transfers between devices, from_chip(): return lax.ppermute(value, CHIPS, pairs)  26.5 us
    unnamed x114, local copies, waits for them, and re-layouts  20.9 us
    ppermute x20, waiting for transfers between devices, from_core(): return lax.ppermute(value, 'c', [(0, 1), (1, 0)])  20.6 us
    reduce_scatter x1, waiting for transfers between devices, local(): lax.psum_scatter(late_grad.reshape(-1, s.cell), PLANE, scatter_dimension=...  18.8 us
    ppermute x1, waiting for transfers between devices, local(): lines = lax.ppermute(late_grad[mlp_end:], AXES, home)  17.3 us
    all_to_all x1, starting transfers between devices, local(): owned = lax.all_to_all(owned, AXES, 0, 0, tiled=True)  9.76 us
  transfers between devices with their start and end apart: 55, of which 28 were waited for; matrix products, arithmetic and copies ran while one was open for 3% of the time, Pallas kernels for 20%

commit v1 on v0

--- a/solution.py
+++ b/solution.py
@@ -813,7 +813,7 @@
         name="place_weights",
     )
     early = lax.all_gather(early, PLANE, axis=0)
-    (cotangent_then,) = tie([cotangent], [Far(input_near[1])], "cotangent_then", HBM)
+    (cotangent_then,) = tie([cotangent], [tokens_then], "cotangent_then", HBM)
     upstream_near = from_chips(cotangent_then)
     slots, sequence, position = layout(table, other_table)
     freq = THETA ** (-(2.0 * jnp.arange(HEAD_SIZE // 2, dtype=F32)) / HEAD_SIZE)

time: 433 us -> 433 us (level)
  starting transfers between devices: 69.6 us -> 78.1 us
  waiting for transfers between devices: 189 us -> 181 us
    ppermute x24, waiting for transfers between devices: 111 us -> 103 us  [from_chip(): return lax.ppermute(value, CHIPS, pairs)]
    ppermute x24, starting transfers between devices: 26.5 us -> 31.5 us  [from_chip(): return lax.ppermute(value, CHIPS, pairs)]
    unnamed x114 -> x108, local copies, waits for them, and re-layouts: 20.9 us -> 19.6 us
  transfers between devices with their start and end apart: 55 -> 55, of which waited for: 28 -> 30; matrix products, arithmetic and copies ran while one was open for 3% -> 3% of each run, Pallas kernels for 20% -> 20%
where the time goes in v1:
time: 433 us; the launch traced here: 426 us
  waiting for transfers between devices  181 us (42%)
  Pallas kernels  121 us (28%)
  starting transfers between devices  78.1 us (18%)
  local copies, waits for them, and re-layouts  24.3 us (6%)
  between operations  14.6 us (3%)
  other arithmetic  6.75 us (2%)
    pallas_call x19, Pallas kernels, call(): pl.pallas_call(run, out_shape=tuple(outs), in_specs=in_specs + after_spec...  121 us
    ppermute x24, waiting for transfers between devices, from_chip(): return lax.ppermute(value, CHIPS, pairs)  103 us
    ppermute x24, starting transfers between devices, from_chip(): return lax.ppermute(value, CHIPS, pairs)  31.5 us
    unnamed x108, local copies, waits for them, and re-layouts  19.6 us
    reduce_scatter x1, waiting for transfers between devices, local(): lax.psum_scatter(late_grad.reshape(-1, s.cell), PLANE, scatter_dimension=...  19.1 us
    ppermute x20, waiting for transfers between devices, from_core(): return lax.ppermute(value, 'c', [(0, 1), (1, 0)])  19 us
    ppermute x1, waiting for transfers between devices, local(): lines = lax.ppermute(late_grad[mlp_end:], AXES, home)  17.3 us
    all_to_all x1, starting transfers between devices, local(): owned = lax.all_to_all(owned, AXES, 0, 0, tiled=True)  9.68 us
  transfers between devices with their start and end apart: 55, of which 30 were waited for; matrix products, arithmetic and copies ran while one was open for 3% of the time, Pallas kernels for 20%

profile of v1, /device:TPU:6, one launch (start us, length us, event | category | flops | bytes accessed | tf_op | source)
XLA Modules:
  0.0 425.8 jit_solution(17203171215111998020)
XLA Ops:
  7.2 3.1 pack_weights.1
  10.4 4.9 %all-to-all-start = ((bf16[8,80,512]{2,1,0:T(8,128)(2,1)}), bf16[8,80,512]{2,1,0:T(8,128)(2,1)S(1)}, u32[]{:S(2)}, u32[]{:S(2)}) async-start(bf16[8,80,512]{2,1,0:T(8,128)(2,1)} %get-tuple-element.110), calls=%async_computation | async-start | bytes 1310720 | tf_op jit(solution)/shard_map/all_to_all | solution.py:800
  15.3 4.6 %collective-permute-start.7 = (bf16[256,512]{1,0:T(8,128)(2,1)}, bf16[256,512]{1,0:T(8,128)(2,1)S(1)}, u32[]{:S(2)}, u32[]{:S(2)}) collective-permute-start(bf16[256,512]{1,0:T(8,128)(2,1)} %get-tuple-element.111), channel_id=1, source_target_pairs={{0,0},{1,4},{2,8},{3,12},{4,32},{5,36},{6,40},{7,44},{8,64},{9,68}... | collective-permute-start | bytes 786440 | tf_op jit(solution)/shard_map/ppermute | solution.py:801
  21.4 8.7 %collective-permute-done.8.refs_2_ = s32[10]{0:T(128)S(1)} collective-permute-done((s32[10]{0:T(128)}, s32[10]{0:T(128)S(1)}, u32[]{:S(2)}, u32[]{:S(2)}) %collective-permute-start.8) | collective-permute-done | bytes 72 | tf_op jit(solution)/shard_map/ppermute | solution.py:796
  30.0 8.6 %collective-permute-done.7.refs_1_ = bf16[256,512]{1,0:T(8,128)(2,1)S(1)} collective-permute-done((bf16[256,512]{1,0:T(8,128)(2,1)}, bf16[256,512]{1,0:T(8,128)(2,1)S(1)}, u32[]{:S(2)}, u32[]{:S(2)}) %collective-permute-start.7) | collective-permute-done | bytes 262176 | tf_op jit(solution)/shard_map/ppermute | solution.py:801
  41.9 2.0 collective-permute-start.21
  47.9 9.0 %collective-permute-done.22.refs_10_.refs_11_ = bf16[128,2048]{1,0:T(8,128)(2,1)S(1)} collective-permute-done((bf16[128,2048]{1,0:T(8,128)(2,1)}, bf16[128,2048]{1,0:T(8,128)(2,1)S(1)}, u32[]{:S(2)}, u32[]{:S(2)}) %collective-permute-start.22) | collective-permute-done | bytes 524320 | tf_op jit(solution)/shard_map/ppermute | solution.py:45
  58.2 10.1 %collective-permute-done.2.refs_3_ = bf16[128,2048]{1,0:T(8,128)(2,1)} collective-permute-done((bf16[128,2048]{1,0:T(8,128)(2,1)}, bf16[128,2048]{1,0:T(8,128)(2,1)}, u32[]{:S(2)}, u32[]{:S(2)}) %collective-permute-start.2) | collective-permute-done | bytes 524320 | tf_op jit(solution)/shard_map/ppermute | solution.py:45
  68.8 10.3 %collective-permute-done.refs_1_ = bf16[128,2048]{1,0:T(8,128)(2,1)} collective-permute-done((bf16[128,2048]{1,0:T(8,128)(2,1)}, bf16[128,2048]{1,0:T(8,128)(2,1)}, u32[]{:S(2)}, u32[]{:S(2)}) %collective-permute-start) | collective-permute-done | bytes 524320 | tf_op jit(solution)/shard_map/ppermute | solution.py:45
  83.9 2.4 collective-permute-done.20.refs_8_.refs_9_
  86.5 2.9 all-gather.5.cloned.1.call-done
  91.6 14.0 %head_forward.1 = (bf16[2048,512]{1,0:T(8,128)(2,1)}, bf16[256,2048]{1,0:T(8,128)(2,1)}, bf16[1024,2048]{1,0:T(8,128)(2,1)}, f32[1024,384]{1,0:T(8,128)}, f32[4,...) custom-call(bf16[128,2048]{1,0:T(8,128)(2,1)} %tokens_then.1.refs_0_, ...), custom_call_target="tpu_custom_call" | custom-call | flops 3221225472 | bytes 29631488 | tf_op jit(solution)/shard_map/head_forward/pallas_call | solution.py:192
  105.6 4.4 %collective-permute-done.9.refs_1_ = bf16[512,2048]{1,0:T(8,128)(2,1)S(1)} collective-permute-done((bf16[512,2048]{1,0:T(8,128)(2,1)}, bf16[512,2048]{1,0:T(8,128)(2,1)S(1)}, u32[]{:S(2)}, u32[]{:S(2)}) %collective-permute-start.9) | collective-permute-done | bytes 2097184 | tf_op jit(solution)/shard_map/ppermute | solution.py:49
  112.0 6.7 %collective-permute-start.10 = (bf16[128,2048]{1,0:T(8,128)(2,1)S(1)}, bf16[128,2048]{1,0:T(8,128)(2,1)S(1)}, u32[]{:S(2)}, u32[]{:S(2)}) collective-permute-start(bf16[128,2048]{1,0:T(8,128)(2,1)S(1)} %get-tuple-element.116), channel_id=1, source_target_pairs={{2,0},{18,16},{0,2},{16,18},{3,1},{19,17},{1,3},{17,19},{6,4},{22,... | collective-permute-start | bytes 1572872 | tf_op jit(solution)/shard_map/ppermute | solution.py:45
  121.3 10.2 %collective-permute-done.10.refs_1_ = bf16[128,2048]{1,0:T(8,128)(2,1)S(1)} collective-permute-done((bf16[128,2048]{1,0:T(8,128)(2,1)S(1)}, bf16[128,2048]{1,0:T(8,128)(2,1)S(1)}, u32[]{:S(2)}, u32[]{:S(2)}) %collective-permute-start.10) | collective-permute-done | bytes 524320 | tf_op jit(solution)/shard_map/ppermute | solution.py:45
  131.6 8.2 %collective-permute-done.11.refs_2_ = bf16[128,2048]{1,0:T(8,128)(2,1)S(1)} collective-permute-done((bf16[128,2048]{1,0:T(8,128)(2,1)S(1)}, bf16[128,2048]{1,0:T(8,128)(2,1)S(1)}, u32[]{:S(2)}, u32[]{:S(2)}) %collective-permute-start.11) | collective-permute-done | bytes 524320 | tf_op jit(solution)/shard_map/ppermute | solution.py:45
  139.8 2.4 collective-permute-done.12.refs_3_
  144.9 3.2 collective-permute-start.13
  148.7 9.0 %collective-permute-done.15.refs_3_ = bf16[128,2048]{1,0:T(8,128)(2,1)S(1)} collective-permute-done((bf16[128,2048]{1,0:T(8,128)(2,1)S(1)}, bf16[128,2048]{1,0:T(8,128)(2,1)S(1)}, u32[]{:S(2)}, u32[]{:S(2)}) %collective-permute-start.15) | collective-permute-done | bytes 524320 | tf_op jit(solution)/shard_map/ppermute | solution.py:45
  158.6 12.4 %collective-permute-done.13.refs_1_ = bf16[128,2048]{1,0:T(8,128)(2,1)S(1)} collective-permute-done((bf16[128,2048]{1,0:T(8,128)(2,1)S(1)}, bf16[128,2048]{1,0:T(8,128)(2,1)S(1)}, u32[]{:S(2)}, u32[]{:S(2)}) %collective-permute-start.13) | collective-permute-done | bytes 524320 | tf_op jit(solution)/shard_map/ppermute | solution.py:45
  173.1 26.1 %mlp_block.1 = (bf16[768,2048]{1,0:T(8,128)(2,1)}, bf16[1024,768]{1,0:T(8,128)(2,1)}, bf16[1024,1536]{1,0:T(8,128)(2,1)}, bf16[512,2048]{1,0:T(8,128)(2,1)}, bf16[512,2048]{1,0:T(8,128)(2,1)}) custom-call(bf16[128,2048]{1,0:T(8,128)(2,1)} %copy-done.22, bf16[128,2048]{1,0:T(8,128)(2,1)} %copy-done.45, bf16[128,2048]{1,0:T(8,128)(2,1)} %copy-done.44, ...), custom_call_target="tpu_custom_call" | custom-call | flops 16106127360 | bytes 29884416 | tf_op jit(solution)/shard_map/mlp_block/pallas_call | solution.py:192
  199.7 4.0 collective-permute-done.27.refs_1_
  206.7 2.1 collective-permute-start.29
  208.7 18.5 %mlp_weight_grads.1 = (bf16[16,576,512]{2,1,0:T(8,128)(2,1)}, f32[8,128]{1,0:T(8,128)}) custom-call(bf16[128,2048]{1,0:T(8,128)(2,1)} %copy-done.22, bf16[128,2048]{1,0:T(8,128)(2,1)} %copy-done.45, bf16[128,2048]{1,0:T(8,128)(2,1)} %copy-done.44, bf16[128,2048]{1,0:T(8,128)(2,1)} %copy-done.43, bf16[128,2048]{1,0:T(8,128)(2,1)} %copy-done.47, ...), custom_call_target="tpu_custom_call" | custom-call | flops 9663676416 | bytes 22548480 | tf_op jit(solution)/shard_map/mlp_weight_grads/pallas_call | solution.py:192
  227.3 2.6 collective-permute-done.29.refs_2_
  229.9 2.9 collective-permute-done.30.refs_3_
  239.8 7.2 %mlp_out.1 = (bf16[512,2048]{1,0:T(8,128)(2,1)}, bf16[512,2048]{1,0:T(8,128)(2,1)}) custom-call(bf16[1024,768]{1,0:T(8,128)(2,1)} %get-tuple-element.121.refs_17_.refs_0_, bf16[768,2048]{1,0:T(8,128)(2,1)} %get-tuple-element.122.refs_1_, bf16[128,2048]{1,0:T(8,128)(2,1)} %get-tuple-element.132.refs_2_.refs_0_.refs_1_), custom_call_target="tpu_custom_call" | custom-call | flops 3221225472 | bytes 8912896 | tf_op jit(solution)/shard_map/mlp_out/pallas_call | solution.py:192
  247.0 5.0 %collective-permute-done.33.refs_3_ = bf16[128,2048]{1,0:T(8,128)(2,1)S(1)} collective-permute-done((bf16[128,2048]{1,0:T(8,128)(2,1)}, bf16[128,2048]{1,0:T(8,128)(2,1)S(1)}, u32[]{:S(2)}, u32[]{:S(2)}) %collective-permute-start.33) | collective-permute-done | bytes 524320 | tf_op jit(solution)/shard_map/ppermute | solution.py:45
  252.0 11.8 %collective-permute-done.32.refs_2_ = bf16[128,2048]{1,0:T(8,128)(2,1)S(1)} collective-permute-done((bf16[128,2048]{1,0:T(8,128)(2,1)}, bf16[128,2048]{1,0:T(8,128)(2,1)S(1)}, u32[]{:S(2)}, u32[]{:S(2)}) %collective-permute-start.32) | collective-permute-done | bytes 524320 | tf_op jit(solution)/shard_map/ppermute | solution.py:45
  265.6 3.7 collective-permute-done.38.refs_4_
  272.8 5.6 %out_weight_grads.1 = bf16[256,2048]{1,0:T(8,128)(2,1)} custom-call(bf16[128,2048]{1,0:T(8,128)(2,1)} %get-tuple-element.132.refs_2_.refs_0_.refs_1_, bf16[128,2048]{1,0:T(8,128)(2,1)} %get-tuple-element.140.refs_1_, bf16[128,2048]{1,0:T(8,128)(2,1)} %get-tuple-element.141.refs_2_, bf16[128,2048]{1,0:T(8,128)(2,1)} %get-tuple-element.142.refs_3_, ...), custom_call_target="tpu_custom_call" | custom-call | flops 1073741824 | bytes 5767168 | tf_op jit(solution)/shard_map/out_weight_grads/pallas_call | solution.py:192
  278.4 9.6 %all-to-all-start.1 = ((bf16[16,16,2048]{2,1,0:T(8,128)(2,1)}), bf16[16,16,2048]{2,1,0:T(8,128)(2,1)S(1)}, u32[]{:S(2)}, u32[]{:S(2)}) async-start(bf16[16,16,2048]{2,1,0:T(8,128)(2,1)} %bitcast.26), calls=%async_computation.1 | async-start | bytes 2097152 | tf_op jit(solution)/shard_map/all_to_all | solution.py:950
  289.6 2.8 output_add.1
  294.3 2.4 collective-permute-start.37
  296.8 21.8 %head_back.1 = (bf16[512,2048]{1,0:T(8,128)(2,1)}, bf16[512,2048]{1,0:T(8,128)(2,1)}, bf16[128,16,640]{2,1,0:T(8,128)(2,1)}, f32[8,128]{1,0:T(8,128)}) custom-call(bf16[128,2048]{1,0:T(8,128)(2,1)} %get-tuple-element.132.refs_2_.refs_0_.refs_1_, bf16[128,2048]{1,0:T(8,128)(2,1)} %get-tuple-element.140.refs_1_, bf16[128,2048]{1,0:T(8,128)(2,1)} %get-tuple-element.141.refs_2_, ...), custom_call_target="tpu_custom_call" | custom-call | tf_op jit(solution)/shard_map/head_back/pallas_call | solution.py:192
  321.3 2.7 output_end.1.refs_2_
  324.1 9.7 %all-to-all-start.2 = ((bf16[128,16,640]{2,1,0:T(8,128)(2,1)}), bf16[128,16,640]{2,1,0:T(8,128)(2,1)}, u32[]{:S(2)}, u32[]{:S(2)}) async-start(bf16[128,16,640]{2,1,0:T(8,128)(2,1)} %get-tuple-element.164), calls=%async_computation.2 | async-start | bytes 5242880 | tf_op jit(solution)/shard_map/all_to_all | solution.py:978
  334.0 4.2 collective-permute-done.42.refs_1_
  344.1 19.1 %reduce-scatter.2.cloned.1.call-done.refs_0_ = bf16[576,512]{1,0:T(8,128)(2,1)} async-done(((bf16[9216,512]{1,0:T(8,128)(2,1)}), bf16[576,512]{1,0:T(8,128)(2,1)}) %reduce-scatter.2.cloned.1.call-update) | async-done | bytes 589840 | tf_op jit(solution)/shard_map/reduce_scatter | solution.py:923
  365.0 3.0 all-to-all-done.2.refs_11_.refs_0_
  368.0 5.8 %all-to-all-start.3 = ((bf16[8,48,512]{2,1,0:T(8,128)(2,1)}), bf16[8,48,512]{2,1,0:T(8,128)(2,1)}, u32[]{:S(2)}, u32[]{:S(2)}) async-start(bf16[8,48,512]{2,1,0:T(8,128)(2,1)} %bitcast.27), calls=%async_computation.4 | async-start | bytes 786432 | tf_op jit(solution)/shard_map/all_to_all | solution.py:987
  374.8 3.0 collective-permute-start.47
  377.7 4.6 %collective-permute-start.46 = (bf16[16,2048]{1,0:T(8,128)(2,1)S(1)}, bf16[16,2048]{1,0:T(8,128)(2,1)S(1)}, u32[]{:S(2)}, u32[]{:S(2)}) collective-permute-start(bf16[16,2048]{1,0:T(8,128)(2,1)S(1)} %copy-done.16), channel_id=1, source_target_pairs={{0,0},{4,1},{8,2},{12,3},{32,4},{36,5},{40,6},{44,7},{64,8},{68,9}... | collective-permute-start | bytes 196616 | tf_op jit(solution)/shard_map/ppermute | solution.py:989
  382.4 3.9 collective-permute-done.43.refs_1_
  386.3 3.1 input_end.1
  390.0 17.3 %collective-permute-done.47.refs_1_ = bf16[192,512]{1,0:T(8,128)(2,1)S(1)} collective-permute-done((bf16[192,512]{1,0:T(8,128)(2,1)S(1)}, bf16[192,512]{1,0:T(8,128)(2,1)S(1)}, u32[]{:S(2)}, u32[]{:S(2)}) %collective-permute-start.47) | collective-permute-done | bytes 196640 | tf_op jit(solution)/shard_map/ppermute | solution.py:988
  408.0 5.3 %mlp_update.1 = (f32[16,6144]{1,0:T(8,128)}, f32[16,6144]{1,0:T(8,128)}, f32[16,6144]{1,0:T(8,128)}, f32[16,6144]{1,0:T(8,128)}, f32[16,6144]{1,0:T(8,128)}, /*i...) custom-call(bf16[8,48,512]{2,1,0:T(8,128)(2,1)} %all-to-all-done.3.refs, ...), custom_call_target="tpu_custom_call" | custom-call | bytes 7671808 | tf_op jit(solution)/shard_map/mlp_update/pallas_call | solution.py:192
  414.0 5.1 %head_update.1 = (f32[16,2048]{1,0:T(8,128)}, f32[16,2048]{1,0:T(8,128)}, f32[16,2048]{1,0:T(8,128)}, f32[16,1024]{1,0:T(8,128)}, f32[16,1024]{1,0:T(8,128)}, /*...) custom-call(bf16[128,16,640]{2,1,0:T(8,128)(2,1)} %all-to-all-done.2, ...), custom_call_target="tpu_custom_call" | custom-call | bytes 5047088 | tf_op jit(solution)/shard_map/head_update/pallas_call | solution.py:192
  (235 shorter events, 61.0 us)
Async XLA Ops:
  10.4 28.2 %all-to-all-start = ((bf16[8,80,512]{2,1,0:T(8,128)(2,1)}), bf16[8,80,512]{2,1,0:T(8,128)(2,1)S(1)}, u32[]{:S(2)}, u32[]{:S(2)}) async-start(bf16[8,80,512]{2,1,0:T(8,128)(2,1)} %get-tuple-element.110), calls=%async_computation | async-start | bytes 1310720 | tf_op jit(solution)/shard_map/all_to_all | solution.py:800
  15.3 74.1 %all-gather.5.cloned.1.call-start = ((), (), s32[]{:S(2)}) async-start(), calls=%async_computation.6 | async-start | bytes 3620864 | tf_op jit(solution)/shard_map/all_gather | solution.py:815
  15.3 23.3 %collective-permute-start.7 = (bf16[256,512]{1,0:T(8,128)(2,1)}, bf16[256,512]{1,0:T(8,128)(2,1)S(1)}, u32[]{:S(2)}, u32[]{:S(2)}) collective-permute-start(bf16[256,512]{1,0:T(8,128)(2,1)} %get-tuple-element.111), channel_id=1, source_target_pairs={{0,0},{1,4},{2,8},{3,12},{4,32},{5,36},{6,40},{7,44},{8,64},{9,68}... | collective-permute-start | bytes 786440 | tf_op jit(solution)/shard_map/ppermute | solution.py:801
  20.6 9.5 %collective-permute-start.8 = (s32[10]{0:T(128)}, s32[10]{0:T(128)S(1)}, u32[]{:S(2)}, u32[]{:S(2)}) collective-permute-start(s32[10]{0:T(128)} %table_then.1), channel_id=1, source_target_pairs={{0,16},{16,0},{1,17},{17,1},{2,18},{18,2},{3,19},{19,3},{4,20},{20... | collective-permute-start | bytes 128 | tf_op jit(solution)/shard_map/ppermute | solution.py:796
  40.2 132.9 %all-gather.7.cloned.1.call-start = ((), (), s32[]{:S(2)}) async-start(), calls=%async_computation.7 | async-start | bytes 10027008 | tf_op jit(solution)/shard_map/all_gather | solution.py:830
  41.9 15.1 %collective-permute-start.22 = (bf16[128,2048]{1,0:T(8,128)(2,1)}, bf16[128,2048]{1,0:T(8,128)(2,1)S(1)}, u32[]{:S(2)}, u32[]{:S(2)}) collective-permute-start(bf16[128,2048]{1,0:T(8,128)(2,1)} %cotangent_then.1.refs_8_), channel_id=1, source_target_pairs={{18,0},{0,16},{16,2},{2,18},{19,1},{1,17},{17,3},{3,19},{22,4},{4,... | collective-permute-start | bytes 1572872 | tf_op jit(solution)/shard_map/ppermute | solution.py:45
  41.9 16.3 %collective-permute-start.21 = (bf16[128,2048]{1,0:T(8,128)(2,1)}, bf16[128,2048]{1,0:T(8,128)(2,1)S(1)}, u32[]{:S(2)}, u32[]{:S(2)}) collective-permute-start(bf16[128,2048]{1,0:T(8,128)(2,1)} %cotangent_then.1.refs_8_), channel_id=1, source_target_pairs={{16,0},{2,16},{18,2},{0,18},{17,1},{3,17},{19,3},{1,19},{20,4},{6,... | collective-permute-start | bytes 1572872 | tf_op jit(solution)/shard_map/ppermute | solution.py:45
  43.9 24.4 %collective-permute-start.2 = (bf16[128,2048]{1,0:T(8,128)(2,1)}, bf16[128,2048]{1,0:T(8,128)(2,1)}, u32[]{:S(2)}, u32[]{:S(2)}) collective-permute-start(bf16[128,2048]{1,0:T(8,128)(2,1)} %tokens_then.1.refs_0_.refs_1_), channel_id=1, source_target_pairs={{18,0},{0,16},{16,2},{2,18},{19,1},{1,17},{17,3},{3,19},{22,4},{4,... | collective-permute-start | bytes 1572872 | tf_op jit(solution)/shard_map/ppermute | solution.py:45
  45.1 23.2 %collective-permute-start.1 = (bf16[128,2048]{1,0:T(8,128)(2,1)}, bf16[128,2048]{1,0:T(8,128)(2,1)}, u32[]{:S(2)}, u32[]{:S(2)}) collective-permute-start(bf16[128,2048]{1,0:T(8,128)(2,1)} %tokens_then.1.refs_0_.refs_1_), channel_id=1, source_target_pairs={{16,0},{2,16},{18,2},{0,18},{17,1},{3,17},{19,3},{1,19},{20,4},{6,... | collective-permute-start | bytes 1572872 | tf_op jit(solution)/shard_map/ppermute | solution.py:45
  45.9 33.2 %collective-permute-start = (bf16[128,2048]{1,0:T(8,128)(2,1)}, bf16[128,2048]{1,0:T(8,128)(2,1)}, u32[]{:S(2)}, u32[]{:S(2)}) collective-permute-start(bf16[128,2048]{1,0:T(8,128)(2,1)} %tokens_then.1.refs_0_.refs_1_), channel_id=1, source_target_pairs={{2,0},{18,16},{0,2},{16,18},{3,1},{19,17},{1,3},{17,19},{6,4},{22,... | collective-permute-start | bytes 1572872 | tf_op jit(solution)/shard_map/ppermute | solution.py:45
  56.9 29.3 %collective-permute-start.20 = (bf16[128,2048]{1,0:T(8,128)(2,1)}, bf16[128,2048]{1,0:T(8,128)(2,1)}, u32[]{:S(2)}, u32[]{:S(2)}) collective-permute-start(bf16[128,2048]{1,0:T(8,128)(2,1)} %cotangent_then.1.refs_8_), channel_id=1, source_target_pairs={{2,0},{18,16},{0,2},{16,18},{3,1},{19,17},{1,3},{17,19},{6,4},{22,... | collective-permute-start | bytes 1572872 | tf_op jit(solution)/shard_map/ppermute | solution.py:45
  58.2 28.1 %collective-permute-start.3 = (bf16[128,2048]{1,0:T(8,128)(2,1)}, bf16[128,2048]{1,0:T(8,128)(2,1)}, u32[]{:S(2)}, u32[]{:S(2)}) collective-permute-start(bf16[128,2048]{1,0:T(8,128)(2,1)} %tokens_then.1.refs_0_.refs_1_), channel_id=1, source_target_pairs={{0,1},{1,0},{2,3},{3,2},{4,5},{5,4},{6,7},{7,6},{8,9},{9,8},{10,11... | collective-permute-start | bytes 1572872 | tf_op jit(solution)/shard_map/ppermute | solution.py:49
  68.3 18.0 %collective-permute-start.6 = (bf16[128,2048]{1,0:T(8,128)(2,1)}, bf16[128,2048]{1,0:T(8,128)(2,1)}, u32[]{:S(2)}, u32[]{:S(2)}) collective-permute-start(bf16[128,2048]{1,0:T(8,128)(2,1)} %collective-permute-done.2.refs_3_), channel_id=1, source_target_pairs={{0,1},{1,0},{2,3},{3,2},{4,5},{5,4},{6,7},{7,6},{8,9},{9,8},{10,11... | collective-permute-start | bytes 1572872 | tf_op jit(solution)/shard_map/ppermute | solution.py:49
  68.3 18.0 %collective-permute-start.5 = (bf16[128,2048]{1,0:T(8,128)(2,1)}, bf16[128,2048]{1,0:T(8,128)(2,1)}, u32[]{:S(2)}, u32[]{:S(2)}) collective-permute-start(bf16[128,2048]{1,0:T(8,128)(2,1)} %collective-permute-done.1.refs_2_), channel_id=1, source_target_pairs={{0,1},{1,0},{2,3},{3,2},{4,5},{5,4},{6,7},{7,6},{8,9},{9,8},{10,11... | collective-permute-start | bytes 1572872 | tf_op jit(solution)/shard_map/ppermute | solution.py:49
  79.1 7.2 %collective-permute-start.4 = (bf16[128,2048]{1,0:T(8,128)(2,1)}, bf16[128,2048]{1,0:T(8,128)(2,1)}, u32[]{:S(2)}, u32[]{:S(2)}) collective-permute-start(bf16[128,2048]{1,0:T(8,128)(2,1)} %collective-permute-done.refs_1_), channel_id=1, source_target_pairs={{0,1},{1,0},{2,3},{3,2},{4,5},{5,4},{6,7},{7,6},{8,9},{9,8},{10,11... | collective-permute-start | bytes 1572872 | tf_op jit(solution)/shard_map/ppermute | solution.py:49
  86.3 276.9 %reduce-scatter.2.cloned.1.call-start = ((), (), s32[]{:S(2)}) async-start(), calls=%async_computation.5 | async-start | bytes 10027008 | tf_op jit(solution)/shard_map/reduce_scatter | solution.py:923
  112.0 19.5 %collective-permute-start.10 = (bf16[128,2048]{1,0:T(8,128)(2,1)S(1)}, bf16[128,2048]{1,0:T(8,128)(2,1)S(1)}, u32[]{:S(2)}, u32[]{:S(2)}) collective-permute-start(bf16[128,2048]{1,0:T(8,128)(2,1)S(1)} %get-tuple-element.116), channel_id=1, source_target_pairs={{2,0},{18,16},{0,2},{16,18},{3,1},{19,17},{1,3},{17,19},{6,4},{22,... | collective-permute-start | bytes 1572872 | tf_op jit(solution)/shard_map/ppermute | solution.py:45
  118.8 21.0 %collective-permute-start.11 = (bf16[128,2048]{1,0:T(8,128)(2,1)S(1)}, bf16[128,2048]{1,0:T(8,128)(2,1)S(1)}, u32[]{:S(2)}, u32[]{:S(2)}) collective-permute-start(bf16[128,2048]{1,0:T(8,128)(2,1)S(1)} %get-tuple-element.117), channel_id=1, source_target_pairs={{18,0},{0,16},{16,2},{2,18},{19,1},{1,17},{17,3},{3,19},{22,4},{4,... | collective-permute-start | bytes 1572872 | tf_op jit(solution)/shard_map/ppermute | solution.py:45
  119.0 23.2 %collective-permute-start.12 = (bf16[128,2048]{1,0:T(8,128)(2,1)S(1)}, bf16[128,2048]{1,0:T(8,128)(2,1)S(1)}, u32[]{:S(2)}, u32[]{:S(2)}) collective-permute-start(bf16[128,2048]{1,0:T(8,128)(2,1)S(1)} %get-tuple-element.118), channel_id=1, source_target_pairs={{16,0},{2,16},{18,2},{0,18},{17,1},{3,17},{19,3},{1,19},{20,4},{6,... | collective-permute-start | bytes 1572872 | tf_op jit(solution)/shard_map/ppermute | solution.py:45
  120.8 24.1 %collective-permute-start.23 = (bf16[128,2048]{1,0:T(8,128)(2,1)S(1)}, bf16[128,2048]{1,0:T(8,128)(2,1)S(1)}, u32[]{:S(2)}, u32[]{:S(2)}) collective-permute-start(bf16[128,2048]{1,0:T(8,128)(2,1)S(1)} %copy-done.28), channel_id=1, source_target_pairs={{0,1},{1,0},{2,3},{3,2},{4,5},{5,4},{6,7},{7,6},{8,9},{9,8},{10,11... | collective-permute-start | bytes 1572872 | tf_op jit(solution)/shard_map/ppermute | solution.py:49
  120.8 27.3 %collective-permute-start.26 = (bf16[128,2048]{1,0:T(8,128)(2,1)S(1)}, bf16[128,2048]{1,0:T(8,128)(2,1)S(1)}, u32[]{:S(2)}, u32[]{:S(2)}) collective-permute-start(bf16[128,2048]{1,0:T(8,128)(2,1)S(1)} %copy-done.34), channel_id=1, source_target_pairs={{0,1},{1,0},{2,3},{3,2},{4,5},{5,4},{6,7},{7,6},{8,9},{9,8},{10,11... | collective-permute-start | bytes 1572872 | tf_op jit(solution)/shard_map/ppermute | solution.py:49
  131.5 16.6 %collective-permute-start.25 = (bf16[128,2048]{1,0:T(8,128)(2,1)S(1)}, bf16[128,2048]{1,0:T(8,128)(2,1)S(1)}, u32[]{:S(2)}, u32[]{:S(2)}) collective-permute-start(bf16[128,2048]{1,0:T(8,128)(2,1)S(1)} %copy-done.36), channel_id=1, source_target_pairs={{0,1},{1,0},{2,3},{3,2},{4,5},{5,4},{6,7},{7,6},{8,9},{9,8},{10,11... | collective-permute-start | bytes 1572872 | tf_op jit(solution)/shard_map/ppermute | solution.py:49
  142.8 14.8 %collective-permute-start.15 = (bf16[128,2048]{1,0:T(8,128)(2,1)S(1)}, bf16[128,2048]{1,0:T(8,128)(2,1)S(1)}, u32[]{:S(2)}, u32[]{:S(2)}) collective-permute-start(bf16[128,2048]{1,0:T(8,128)(2,1)S(1)} %get-tuple-element.119.refs_0_), channel_id=1, source_target_pairs={{18,0},{0,16},{16,2},{2,18},{19,1},{1,17},{17,3},{3,19},{22,4},{4,... | collective-permute-start | bytes 1572872 | tf_op jit(solution)/shard_map/ppermute | solution.py:45
  143.5 15.1 %collective-permute-start.14 = (bf16[128,2048]{1,0:T(8,128)(2,1)S(1)}, bf16[128,2048]{1,0:T(8,128)(2,1)S(1)}, u32[]{:S(2)}, u32[]{:S(2)}) collective-permute-start(bf16[128,2048]{1,0:T(8,128)(2,1)S(1)} %get-tuple-element.119.refs_0_), channel_id=1, source_target_pairs={{16,0},{2,16},{18,2},{0,18},{17,1},{3,17},{19,3},{1,19},{20,4},{6,... | collective-permute-start | bytes 1572872 | tf_op jit(solution)/shard_map/ppermute | solution.py:45
  144.9 26.1 %collective-permute-start.13 = (bf16[128,2048]{1,0:T(8,128)(2,1)S(1)}, bf16[128,2048]{1,0:T(8,128)(2,1)S(1)}, u32[]{:S(2)}, u32[]{:S(2)}) collective-permute-start(bf16[128,2048]{1,0:T(8,128)(2,1)S(1)} %get-tuple-element.119.refs_0_), channel_id=1, source_target_pairs={{2,0},{18,16},{0,2},{16,18},{3,1},{19,17},{1,3},{17,19},{6,4},{22,... | collective-permute-start | bytes 1572872 | tf_op jit(solution)/shard_map/ppermute | solution.py:45
  148.2 22.9 %collective-permute-start.24 = (bf16[128,2048]{1,0:T(8,128)(2,1)}, bf16[128,2048]{1,0:T(8,128)(2,1)S(1)}, u32[]{:S(2)}, u32[]{:S(2)}) collective-permute-start(bf16[128,2048]{1,0:T(8,128)(2,1)} %collective-permute-done.20.refs_8_.refs_9_), channel_id=1, source_target_pairs={{0,1},{1,0},{2,3},{3,2},{4,5},{5,4},{6,7},{7,6},{8,9},{9,8},{10,11... | collective-permute-start | bytes 1572872 | tf_op jit(solution)/shard_map/ppermute | solution.py:49
  148.2 22.9 %collective-permute-start.16 = (bf16[128,2048]{1,0:T(8,128)(2,1)S(1)}, bf16[128,2048]{1,0:T(8,128)(2,1)S(1)}, u32[]{:S(2)}, u32[]{:S(2)}) collective-permute-start(bf16[128,2048]{1,0:T(8,128)(2,1)S(1)} %get-tuple-element.119.refs_0_), channel_id=1, source_target_pairs={{0,1},{1,0},{2,3},{3,2},{4,5},{5,4},{6,7},{7,6},{8,9},{9,8},{10,11... | collective-permute-start | bytes 1572872 | tf_op jit(solution)/shard_map/ppermute | solution.py:49
  157.7 13.4 %collective-permute-start.19 = (bf16[128,2048]{1,0:T(8,128)(2,1)S(1)}, bf16[128,2048]{1,0:T(8,128)(2,1)S(1)}, u32[]{:S(2)}, u32[]{:S(2)}) collective-permute-start(bf16[128,2048]{1,0:T(8,128)(2,1)S(1)} %collective-permute-done.15.refs_3_), channel_id=1, source_target_pairs={{0,1},{1,0},{2,3},{3,2},{4,5},{5,4},{6,7},{7,6},{8,9},{9,8},{10,11... | collective-permute-start | bytes 1572872 | tf_op jit(solution)/shard_map/ppermute | solution.py:49
  158.6 12.5 %collective-permute-start.18 = (bf16[128,2048]{1,0:T(8,128)(2,1)S(1)}, bf16[128,2048]{1,0:T(8,128)(2,1)S(1)}, u32[]{:S(2)}, u32[]{:S(2)}) collective-permute-start(bf16[128,2048]{1,0:T(8,128)(2,1)S(1)} %collective-permute-done.14.refs_2_), channel_id=1, source_target_pairs={{0,1},{1,0},{2,3},{3,2},{4,5},{5,4},{6,7},{7,6},{8,9},{9,8},{10,11... | collective-permute-start | bytes 1572872 | tf_op jit(solution)/shard_map/ppermute | solution.py:49
  205.8 21.5 %collective-permute-start.28 = (bf16[128,2048]{1,0:T(8,128)(2,1)S(1)}, bf16[128,2048]{1,0:T(8,128)(2,1)S(1)}, u32[]{:S(2)}, u32[]{:S(2)}) collective-permute-start(bf16[128,2048]{1,0:T(8,128)(2,1)S(1)} %get-tuple-element.126.refs_18_), channel_id=1, source_target_pairs={{2,0},{18,16},{0,2},{16,18},{3,1},{19,17},{1,3},{17,19},{6,4},{22,... | collective-permute-start | bytes 1572872 | tf_op jit(solution)/shard_map/ppermute | solution.py:45
  206.7 23.2 %collective-permute-start.29 = (bf16[128,2048]{1,0:T(8,128)(2,1)S(1)}, bf16[128,2048]{1,0:T(8,128)(2,1)S(1)}, u32[]{:S(2)}, u32[]{:S(2)}) collective-permute-start(bf16[128,2048]{1,0:T(8,128)(2,1)S(1)} %get-tuple-element.127.refs_19_), channel_id=1, source_target_pairs={{18,0},{0,16},{16,2},{2,18},{19,1},{1,17},{17,3},{3,19},{22,4},{4,... | collective-permute-start | bytes 1572872 | tf_op jit(solution)/shard_map/ppermute | solution.py:45
  208.7 24.1 %collective-permute-start.30 = (bf16[128,2048]{1,0:T(8,128)(2,1)S(1)}, bf16[128,2048]{1,0:T(8,128)(2,1)S(1)}, u32[]{:S(2)}, u32[]{:S(2)}) collective-permute-start(bf16[128,2048]{1,0:T(8,128)(2,1)S(1)} %get-tuple-element.128.refs_20_), channel_id=1, source_target_pairs={{16,0},{2,16},{18,2},{0,18},{17,1},{3,17},{19,3},{1,19},{20,4},{6,... | collective-permute-start | bytes 1572872 | tf_op jit(solution)/shard_map/ppermute | solution.py:45
  237.0 15.1 %collective-permute-start.33 = (bf16[128,2048]{1,0:T(8,128)(2,1)}, bf16[128,2048]{1,0:T(8,128)(2,1)S(1)}, u32[]{:S(2)}, u32[]{:S(2)}) collective-permute-start(bf16[128,2048]{1,0:T(8,128)(2,1)} %get-tuple-element.132.refs_2_.refs_0_.refs_1_), channel_id=1, source_target_pairs={{18,0},{0,16},{16,2},{2,18},{19,1},{1,17},{17,3},{3,19},{22,4},{4,... | collective-permute-start | bytes 1572872 | tf_op jit(solution)/shard_map/ppermute | solution.py:45
  237.6 26.2 %collective-permute-start.32 = (bf16[128,2048]{1,0:T(8,128)(2,1)}, bf16[128,2048]{1,0:T(8,128)(2,1)S(1)}, u32[]{:S(2)}, u32[]{:S(2)}) collective-permute-start(bf16[128,2048]{1,0:T(8,128)(2,1)} %get-tuple-element.132.refs_2_.refs_0_.refs_1_), channel_id=1, source_target_pairs={{16,0},{2,16},{18,2},{0,18},{17,1},{3,17},{19,3},{1,19},{20,4},{6,... | collective-permute-start | bytes 1572872 | tf_op jit(solution)/shard_map/ppermute | solution.py:45
  239.2 24.6 %collective-permute-start.31 = (bf16[128,2048]{1,0:T(8,128)(2,1)}, bf16[128,2048]{1,0:T(8,128)(2,1)}, u32[]{:S(2)}, u32[]{:S(2)}) collective-permute-start(bf16[128,2048]{1,0:T(8,128)(2,1)} %get-tuple-element.132.refs_2_.refs_0_.refs_1_), channel_id=1, source_target_pairs={{2,0},{18,16},{0,2},{16,18},{3,1},{19,17},{1,3},{17,19},{6,4},{22,... | collective-permute-start | bytes 1572872 | tf_op jit(solution)/shard_map/ppermute | solution.py:45
  264.6 23.3 %collective-permute-start.34 = (bf16[512,2048]{1,0:T(8,128)(2,1)}, bf16[512,2048]{1,0:T(8,128)(2,1)}, u32[]{:S(2)}, u32[]{:S(2)}) collective-permute-start(bf16[512,2048]{1,0:T(8,128)(2,1)} %get-tuple-element.135), channel_id=1, source_target_pairs={{0,1},{1,0},{2,3},{3,2},{4,5},{5,4},{6,7},{7,6},{8,9},{9,8},{10,11... | collective-permute-start | bytes 6291464 | tf_op jit(solution)/shard_map/ppermute | solution.py:49
  265.6 6.3 %collective-permute-start.41 = (bf16[128,2048]{1,0:T(8,128)(2,1)}, bf16[128,2048]{1,0:T(8,128)(2,1)S(1)}, u32[]{:S(2)}, u32[]{:S(2)}) collective-permute-start(bf16[128,2048]{1,0:T(8,128)(2,1)} %get-tuple-element.142.refs_3_), channel_id=1, source_target_pairs={{0,1},{1,0},{2,3},{3,2},{4,5},{5,4},{6,7},{7,6},{8,9},{9,8},{10,11... | collective-permute-start | bytes 1572872 | tf_op jit(solution)/shard_map/ppermute | solution.py:49
  278.4 40.2 %all-to-all-start.1 = ((bf16[16,16,2048]{2,1,0:T(8,128)(2,1)}), bf16[16,16,2048]{2,1,0:T(8,128)(2,1)S(1)}, u32[]{:S(2)}, u32[]{:S(2)}) async-start(bf16[16,16,2048]{2,1,0:T(8,128)(2,1)} %bitcast.26), calls=%async_computation.1 | async-start | bytes 2097152 | tf_op jit(solution)/shard_map/all_to_all | solution.py:950
  293.4 26.6 %collective-permute-start.35 = (bf16[128,2048]{1,0:T(8,128)(2,1)}, bf16[128,2048]{1,0:T(8,128)(2,1)}, u32[]{:S(2)}, u32[]{:S(2)}) collective-permute-start(bf16[128,2048]{1,0:T(8,128)(2,1)} %get-tuple-element.137.refs_24_), channel_id=1, source_target_pairs={{2,0},{18,16},{0,2},{16,18},{3,1},{19,17},{1,3},{17,19},{6,4},{22,... | collective-permute-start | bytes 1572872 | tf_op jit(solution)/shard_map/ppermute | solution.py:45
  294.3 25.7 %collective-permute-start.36 = (bf16[128,2048]{1,0:T(8,128)(2,1)}, bf16[128,2048]{1,0:T(8,128)(2,1)}, u32[]{:S(2)}, u32[]{:S(2)}) collective-permute-start(bf16[128,2048]{1,0:T(8,128)(2,1)} %get-tuple-element.138.refs_25_), channel_id=1, source_target_pairs={{18,0},{0,16},{16,2},{2,18},{19,1},{1,17},{17,3},{3,19},{22,4},{4,... | collective-permute-start | bytes 1572872 | tf_op jit(solution)/shard_map/ppermute | solution.py:45
  294.3 25.7 %collective-permute-start.37 = (bf16[128,2048]{1,0:T(8,128)(2,1)S(1)}, bf16[128,2048]{1,0:T(8,128)(2,1)}, u32[]{:S(2)}, u32[]{:S(2)}) collective-permute-start(bf16[128,2048]{1,0:T(8,128)(2,1)S(1)} %get-tuple-element.139.refs_26_), channel_id=1, source_target_pairs={{16,0},{2,16},{18,2},{0,18},{17,1},{3,17},{19,3},{1,19},{20,4},{6,... | collective-permute-start | bytes 1572872 | tf_op jit(solution)/shard_map/ppermute | solution.py:45
  324.1 44.0 %all-to-all-start.2 = ((bf16[128,16,640]{2,1,0:T(8,128)(2,1)}), bf16[128,16,640]{2,1,0:T(8,128)(2,1)}, u32[]{:S(2)}, u32[]{:S(2)}) async-start(bf16[128,16,640]{2,1,0:T(8,128)(2,1)} %get-tuple-element.164), calls=%async_computation.2 | async-start | bytes 5242880 | tf_op jit(solution)/shard_map/all_to_all | solution.py:978
  340.6 41.8 %collective-permute-start.44 = (bf16[128,2048]{1,0:T(8,128)(2,1)}, bf16[128,2048]{1,0:T(8,128)(2,1)}, u32[]{:S(2)}, u32[]{:S(2)}) collective-permute-start(bf16[128,2048]{1,0:T(8,128)(2,1)} %get-tuple-element.160), channel_id=1, source_target_pairs={{18,0},{0,16},{16,2},{2,18},{19,1},{1,17},{17,3},{3,19},{22,4},{4,... | collective-permute-start | bytes 1572872 | tf_op jit(solution)/shard_map/ppermute | solution.py:45
  341.8 40.6 %collective-permute-start.45 = (bf16[128,2048]{1,0:T(8,128)(2,1)}, bf16[128,2048]{1,0:T(8,128)(2,1)}, u32[]{:S(2)}, u32[]{:S(2)}) collective-permute-start(bf16[128,2048]{1,0:T(8,128)(2,1)} %get-tuple-element.161), channel_id=1, source_target_pairs={{16,0},{2,16},{18,2},{0,18},{17,1},{3,17},{19,3},{1,19},{20,4},{6,... | collective-permute-start | bytes 1572872 | tf_op jit(solution)/shard_map/ppermute | solution.py:45
  342.7 43.7 %collective-permute-start.43 = (bf16[128,2048]{1,0:T(8,128)(2,1)S(1)}, bf16[128,2048]{1,0:T(8,128)(2,1)}, u32[]{:S(2)}, u32[]{:S(2)}) collective-permute-start(bf16[128,2048]{1,0:T(8,128)(2,1)S(1)} %get-tuple-element.159.refs_1_), channel_id=1, source_target_pairs={{2,0},{18,16},{0,2},{16,18},{3,1},{19,17},{1,3},{17,19},{6,4},{22,... | collective-permute-start | bytes 1572872 | tf_op jit(solution)/shard_map/ppermute | solution.py:45
  368.0 39.3 %all-to-all-start.3 = ((bf16[8,48,512]{2,1,0:T(8,128)(2,1)}), bf16[8,48,512]{2,1,0:T(8,128)(2,1)}, u32[]{:S(2)}, u32[]{:S(2)}) async-start(bf16[8,48,512]{2,1,0:T(8,128)(2,1)} %bitcast.27), calls=%async_computation.4 | async-start | bytes 786432 | tf_op jit(solution)/shard_map/all_to_all | solution.py:987
  374.8 32.6 %collective-permute-start.47 = (bf16[192,512]{1,0:T(8,128)(2,1)S(1)}, bf16[192,512]{1,0:T(8,128)(2,1)S(1)}, u32[]{:S(2)}, u32[]{:S(2)}) collective-permute-start(bf16[192,512]{1,0:T(8,128)(2,1)S(1)} %slice.42), channel_id=1, source_target_pairs={{0,0},{4,1},{8,2},{12,3},{32,4},{36,5},{40,6},{44,7},{64,8},{68,9}... | collective-permute-start | bytes 589832 | tf_op jit(solution)/shard_map/ppermute | solution.py:988
  377.7 35.6 %collective-permute-start.46 = (bf16[16,2048]{1,0:T(8,128)(2,1)S(1)}, bf16[16,2048]{1,0:T(8,128)(2,1)S(1)}, u32[]{:S(2)}, u32[]{:S(2)}) collective-permute-start(bf16[16,2048]{1,0:T(8,128)(2,1)S(1)} %copy-done.16), channel_id=1, source_target_pairs={{0,0},{4,1},{8,2},{12,3},{32,4},{36,5},{40,6},{44,7},{64,8},{68,9}... | collective-permute-start | bytes 196616 | tf_op jit(solution)/shard_map/ppermute | solution.py:989
  (59 other events, 605.4 us)
Sparse Core Ops, SparseCore 0:
  40.3 49.0 all-gather.4
  91.6 80.8 all-gather.6
  237.1 126.1 reduce-scatter.1
